TPU v7x, 32 devices: a whole 2x2x4 slice. The times are simulated.
32 devices in a mesh: ctx: 16 (over z, x, core), fsdp: 2 (over y).
Axes of the slice: x: 2, y: 2, z: 4, core: 2. Of those that a mesh axis runs over, the one named last changes fastest.
Arguments:
- incoming_sequence: bfloat16 [2, 4096, 768], P('fsdp', 'ctx'), may hold values from -6 to 6
- mixer_scaling_factor: bfloat16 [768], P('fsdp'), may hold values from 0.099609375 to 1.8984375
- asker_lookup_content_maps: bfloat16 [768, 2304], P('fsdp'), may hold values from -0.21875 to 0.21875
- mixer_final_map: bfloat16 [768, 768], P('fsdp'), may hold values from -3.5 to 3.5
- specialist_scaling_factor: bfloat16 [768], P('fsdp'), may hold values from 0.099609375 to 1.8984375
- dispatch_space_map: bfloat16 [768, 16], P('fsdp'), may hold values from -0.0546875 to 0.0546875
- specialist_dispatch_vectors: bfloat16 [16, 16], P('fsdp'), may hold values from -1.5 to 1.5
- specialist_widen_weights_pair: bfloat16 [16, 768, 3072], P('ctx', 'fsdp'), may hold values from -0.21875 to 0.21875
- specialist_shrink_weights_pair: bfloat16 [16, 3072, 768], P('ctx', 'fsdp'), may hold values from -3.5 to 3.5
- document_labels: int32 [2, 4096], P('fsdp', 'ctx'), may hold values from 0 to 7, as said below
- piece_specialist_choice: int32 [2, 4096, 1], P('fsdp', 'ctx'), may hold values from 0 to 15; in each aligned block of 256 rows (0 to 255, 256 to 511, ..., all dimensions but the last counted through in order) at most 32 rows name the same one
- result_cotangent_array: bfloat16 [2, 4096, 768], P('fsdp', 'ctx'), may hold values from -6 to 6
Outputs:
- out: bfloat16 [2, 4096, 768], P('fsdp', 'ctx')
- grad_input: float32 [2, 4096, 768], P('fsdp', 'ctx')
- grad_ln1: float32 [768], P('fsdp')
- grad_qkv: float32 [768, 2304], P('fsdp')
- grad_output_weight: float32 [768, 768], P('fsdp')
- grad_ln2: float32 [768], P('fsdp')
- grad_router: float32 [768, 16], P('fsdp')
- grad_embed: float32 [16, 16], P('fsdp')
- grad_expert_up: float32 [16, 768, 3072], P('ctx', 'fsdp')
- grad_expert_down: float32 [16, 3072, 768], P('ctx', 'fsdp')
Inputs may be any that keep to these rules, and one draw needn't show every extreme that they name: `document_labels`: within a sequence the document numbers never fall. In one sequence, chosen by the seed, all tokens form one document; in each other sequence the numbers run through all of 0 to 7. `piece_specialist_choice`: in each aligned block of 256 tokens of a sequence no expert is named by more than 32 tokens, a bound that some block reaches.
All inputs are finite; a program needn't handle non-finite values.
Results may differ from a plain program's by a relative error of at most 0.02.
Values may be sent and summed in bfloat16 or wider, within the bound.
No kernel may reach another device: no remote copies, remote signals or barrier semaphores. Data moves between devices by JAX's collectives and lax.ppermute only.
A program may use at most 256 MiB of HBM per device.

v0:
```python
import math

import jax
import jax.numpy as jnp
from jax import lax
from jax.sharding import PartitionSpec as P

HD = 64


EPSILON = 1e-05
FLOOR = 0.5
ROUTER_HEAT = 0.5
MATMUL_ACCURACY = lax.Precision.HIGHEST
ROOT_HALF = 0.7071067811865476
ROOT_TWO_PI = 2.5066282746310002
NEG_LARGE = -1e30


def layer_norm(values, gain):
    center = values - jnp.mean(values, axis=-1, keepdims=True)
    spread = jnp.mean(center * center, axis=-1, keepdims=True)
    return center * lax.rsqrt(spread + EPSILON) * gain


def gelu_value(values):
    return 0.5 * values * (1.0 + lax.erf(values * ROOT_HALF))


def gelu_slope(values):
    return (
        0.5 * (1.0 + lax.erf(values * ROOT_HALF))
        + values * jnp.exp(-0.5 * values * values) / ROOT_TWO_PI
    )


def route_gate(normed, router, embed_cols, chosen):
    project = jnp.einsum("...d,dr->...r", normed, router, precision=MATMUL_ACCURACY)
    unit_row_vectors = project / jnp.maximum(
        jnp.sqrt(jnp.sum(project * project, axis=-1, keepdims=True)), FLOOR
    )
    unit_columns = embed_cols / jnp.maximum(
        jnp.sqrt(jnp.sum(embed_cols * embed_cols, axis=0, keepdims=True)), FLOOR
    )
    router_scores = (
        jnp.einsum("...d,dx->...x", unit_row_vectors, unit_columns, precision=MATMUL_ACCURACY)
        / ROUTER_HEAT
    )
    shifted = router_scores - jnp.max(router_scores, axis=-1, keepdims=True)
    raised = jnp.exp(shifted)
    probs = raised / jnp.sum(raised, axis=-1, keepdims=True)
    return jnp.sum(probs * chosen, axis=-1)


def product(left, right, pattern):
    return jnp.einsum(pattern, left, right, preferred_element_type=jnp.float32)


def over_blocks(state, piece_rows, step_fn):
    block_rows = math.gcd(piece_rows, 512)

    def advance(current, block_index):
        return (step_fn(current, block_index * block_rows, block_rows), None)

    final, _ = lax.scan(advance, state, jnp.arange(piece_rows // block_rows, dtype=jnp.int32))
    return final


def mask_for(query_segs, key_segs):
    return key_segs[None, :] == query_segs[:, None]


def keep_same(running):
    return running


def body(
    incoming_sequence,
    mixer_scaling_factor,
    asker_lookup_content_maps,
    mixer_final_map,
    specialist_scaling_factor,
    dispatch_space_map,
    specialist_dispatch_vectors,
    specialist_widen_weights_pair,
    specialist_shrink_weights_pair,
    document_labels,
    piece_specialist_choice,
    result_cotangent_array,
):
    row_count = incoming_sequence.shape[1]
    width = incoming_sequence.shape[2]
    head_count = width // HD
    score_scale = 1.0 / math.sqrt(HD)
    ctx_count = lax.axis_size("ctx")
    fsdp_count = lax.axis_size("fsdp")
    fsdp_at = lax.axis_index("fsdp")
    capacity = max(2, 2 * row_count // ctx_count)
    block_inputs = incoming_sequence[0].astype(jnp.float32)
    picked = piece_specialist_choice[0, :, 0]
    own_segs = document_labels[0]
    seg_low = own_segs[0]
    seg_high = own_segs[row_count - 1]
    gain_in, qkv_full, out_full, gain_mid, router_full, embed_full, up_full = (
        lax.all_gather(mixer_scaling_factor, "fsdp", axis=0, tiled=True),
        lax.all_gather(asker_lookup_content_maps, "fsdp", axis=0, tiled=True),
        lax.all_gather(mixer_final_map, "fsdp", axis=0, tiled=True),
        lax.all_gather(specialist_scaling_factor, "fsdp", axis=0, tiled=True),
        lax.all_gather(dispatch_space_map, "fsdp", axis=0, tiled=True),
        lax.all_gather(specialist_dispatch_vectors, "fsdp", axis=0, tiled=True),
        lax.all_gather(specialist_widen_weights_pair, "fsdp", axis=1, tiled=True),
    )
    seg_all = lax.all_gather(own_segs, "ctx", axis=0, tiled=True)
    gain_in32 = gain_in.astype(jnp.float32)
    normed_input = layer_norm(block_inputs, gain_in32)
    normed_low = normed_input.astype(jnp.bfloat16)
    joined_heads = jnp.dot(normed_low, qkv_full, preferred_element_type=jnp.float32).astype(
        jnp.bfloat16
    )
    query_rows = joined_heads[:, :width]
    key_rows = joined_heads[:, width : 2 * width]
    value_rows = joined_heads[:, 2 * width :]
    query_heads = query_rows.reshape(row_count, head_count, HD)
    key_heads = key_rows.reshape(row_count, head_count, HD)
    value_heads = value_rows.reshape(row_count, head_count, HD)
    start_state = (
        jnp.full((head_count, row_count), NEG_LARGE, jnp.float32),
        jnp.zeros((head_count, row_count), jnp.float32),
        jnp.zeros((head_count, row_count, HD), jnp.float32),
    )
    key_piece = lax.all_gather(key_rows, "ctx", axis=0, tiled=True)
    value_piece = lax.all_gather(value_rows, "ctx", axis=0, tiled=True)

    def forward_step_block(current, offset, block_rows):
        key_segs = lax.dynamic_slice_in_dim(seg_all, offset, block_rows)
        active = (key_segs[block_rows - 1] >= seg_low) & (key_segs[0] <= seg_high)

        def forward_live(running):
            row_top, row_total, context_sum = running
            key_block = lax.dynamic_slice_in_dim(key_piece, offset, block_rows).reshape(
                block_rows, head_count, HD
            )
            value_block = lax.dynamic_slice_in_dim(value_piece, offset, block_rows).reshape(
                block_rows, head_count, HD
            )
            scores = product(query_heads, key_block, "qhd,khd->hqk") * score_scale
            allowed = mask_for(own_segs, key_segs)[None]
            masked = jnp.where(allowed, scores, NEG_LARGE)
            new_top = jnp.maximum(row_top, jnp.max(masked, axis=-1))
            raised = jnp.where(allowed, jnp.exp(masked - new_top[..., None]), 0.0)
            decay = jnp.exp(row_top - new_top)
            row_total = row_total * decay + jnp.sum(raised, axis=-1)
            context_sum = context_sum * decay[..., None] + product(
                raised.astype(jnp.bfloat16), value_block, "hqk,khd->hqd"
            )
            return (new_top, row_total, context_sum)

        return lax.cond(active, forward_live, keep_same, current)

    row_top, row_total, context_sum = over_blocks(
        start_state, key_piece.shape[0], forward_step_block
    )
    log_sum = row_top + jnp.log(row_total)
    context_heads = context_sum / row_total[..., None]
    context_full = jnp.transpose(context_heads, (1, 0, 2)).reshape(row_count, width)
    context_low = context_full.astype(jnp.bfloat16)
    residual_stream = block_inputs + jnp.dot(
        context_low, out_full, preferred_element_type=jnp.float32
    )
    gain_mid32 = gain_mid.astype(jnp.float32)
    normed_mid = layer_norm(residual_stream, gain_mid32)
    mid_low = normed_mid.astype(jnp.bfloat16)
    chosen = (picked[:, None] == jnp.arange(ctx_count, dtype=jnp.int32)[None, :]).astype(
        jnp.float32
    )

    def gate_of(normed, router, embed_cols):
        return route_gate(normed, router, embed_cols, chosen)

    gate, routing_pullback = jax.vjp(
        gate_of,
        mid_low.astype(jnp.float32),
        router_full.astype(jnp.float32),
        embed_full.astype(jnp.float32),
    )
    hits = chosen.astype(jnp.int32)
    slot_rank = jnp.sum(jnp.cumsum(hits, axis=0) * hits, axis=1) - 1
    slot_index = picked * capacity + slot_rank
    send_rows = jnp.zeros((ctx_count * capacity, width), jnp.bfloat16).at[slot_index].set(mid_low)
    arrived = lax.all_to_all(
        send_rows.reshape(ctx_count, capacity, width),
        "ctx",
        split_axis=0,
        concat_axis=0,
        tiled=True,
    ).reshape(ctx_count * capacity, width)
    up_weight = up_full[0]
    down_weight = lax.all_gather(specialist_shrink_weights_pair, "fsdp", axis=1, tiled=True)[0]
    pre_act = jnp.dot(arrived, up_weight, preferred_element_type=jnp.float32)
    hidden = gelu_value(pre_act).astype(jnp.bfloat16)
    made = jnp.dot(hidden, down_weight, preferred_element_type=jnp.float32).astype(jnp.bfloat16)
    returned = lax.all_to_all(
        made.reshape(ctx_count, capacity, width), "ctx", split_axis=0, concat_axis=0, tiled=True
    ).reshape(ctx_count * capacity, width)
    expert_rows = returned[slot_index].astype(jnp.float32)
    result = residual_stream + gate[:, None] * expert_rows
    out_cot = result_cotangent_array[0].astype(jnp.float32)
    grad_gate = jnp.sum(out_cot * expert_rows, axis=1)
    grad_made = (gate[:, None] * out_cot).astype(jnp.bfloat16)
    grad_send = jnp.zeros((ctx_count * capacity, width), jnp.bfloat16).at[slot_index].set(grad_made)
    grad_arrived = lax.all_to_all(
        grad_send.reshape(ctx_count, capacity, width),
        "ctx",
        split_axis=0,
        concat_axis=0,
        tiled=True,
    ).reshape(ctx_count * capacity, width)
    grad_down = product(hidden, grad_arrived, "rf,rd->fd")
    grad_hidden = product(grad_arrived, down_weight, "rd,fd->rf")
    grad_pre = (grad_hidden * gelu_slope(pre_act)).astype(jnp.bfloat16)
    grad_up = product(arrived, grad_pre, "rd,rf->df")
    grad_inputs = product(grad_pre, up_weight, "rf,df->rd").astype(jnp.bfloat16)
    grad_back = lax.all_to_all(
        grad_inputs.reshape(ctx_count, capacity, width),
        "ctx",
        split_axis=0,
        concat_axis=0,
        tiled=True,
    ).reshape(ctx_count * capacity, width)
    grad_routed = grad_back[slot_index].astype(jnp.float32)
    grad_route_in, grad_router_full, grad_embed_full = routing_pullback(grad_gate)
    grad_mid = grad_route_in + grad_routed
    _, mid_back = jax.vjp(layer_norm, residual_stream, gain_mid32)
    grad_from_mid, grad_gain_mid = mid_back(grad_mid)
    grad_residual = out_cot + grad_from_mid
    grad_res_low = grad_residual.astype(jnp.bfloat16)
    grad_out_full = product(context_low, grad_res_low, "rd,re->de")
    grad_context = product(grad_res_low, out_full, "re,de->rd").astype(jnp.bfloat16)
    grad_context_heads = grad_context.reshape(row_count, head_count, HD)
    delta_rows = jnp.sum(
        grad_context_heads.astype(jnp.float32) * jnp.transpose(context_heads, (1, 0, 2)), axis=-1
    )
    lse_rows = jnp.transpose(log_sum)
    lse_all, delta_all = (
        lax.all_gather(lse_rows, "ctx", axis=0, tiled=True),
        lax.all_gather(delta_rows, "ctx", axis=0, tiled=True),
    )
    zero_heads = jnp.zeros((row_count, head_count, HD), jnp.float32)
    query_piece = lax.all_gather(query_rows, "ctx", axis=0, tiled=True)
    grad_piece = lax.all_gather(grad_context, "ctx", axis=0, tiled=True)

    def key_step_block(current, offset, block_rows):
        query_start = offset
        query_segs = lax.dynamic_slice_in_dim(seg_all, query_start, block_rows)
        active = (query_segs[block_rows - 1] >= seg_low) & (query_segs[0] <= seg_high)

        def key_live(running):
            grad_keys, grad_values = running
            query_block = lax.dynamic_slice_in_dim(query_piece, offset, block_rows).reshape(
                block_rows, head_count, HD
            )
            grad_block = lax.dynamic_slice_in_dim(grad_piece, offset, block_rows).reshape(
                block_rows, head_count, HD
            )
            lse_block = jnp.transpose(lax.dynamic_slice_in_dim(lse_all, query_start, block_rows))
            delta_block = jnp.transpose(
                lax.dynamic_slice_in_dim(delta_all, query_start, block_rows)
            )
            scores = product(query_block, key_heads, "qhd,khd->hqk") * score_scale
            allowed = mask_for(query_segs, own_segs)[None]
            probs = jnp.exp(jnp.where(allowed, scores - lse_block[..., None], NEG_LARGE))
            grad_values = grad_values + product(
                probs.astype(jnp.bfloat16), grad_block, "hqk,qhd->khd"
            )
            grad_probs = product(grad_block, value_heads, "qhd,khd->hqk")
            grad_scores = (probs * (grad_probs - delta_block[..., None])).astype(jnp.bfloat16)
            grad_keys = grad_keys + product(grad_scores, query_block, "hqk,qhd->khd") * score_scale
            return (grad_keys, grad_values)

        return lax.cond(active, key_live, keep_same, current)

    grad_keys, grad_values = over_blocks(
        (zero_heads, zero_heads), query_piece.shape[0], key_step_block
    )
    delta_heads = jnp.transpose(delta_rows)
    query_key_piece = lax.all_gather(key_rows, "ctx", axis=0, tiled=True)
    query_value_piece = lax.all_gather(value_rows, "ctx", axis=0, tiled=True)

    def query_step_block(current, offset, block_rows):
        key_segs = lax.dynamic_slice_in_dim(seg_all, offset, block_rows)
        active = (key_segs[block_rows - 1] >= seg_low) & (key_segs[0] <= seg_high)

        def query_live(grad_queries):
            key_block = lax.dynamic_slice_in_dim(query_key_piece, offset, block_rows).reshape(
                block_rows, head_count, HD
            )
            value_block = lax.dynamic_slice_in_dim(query_value_piece, offset, block_rows).reshape(
                block_rows, head_count, HD
            )
            scores = product(query_heads, key_block, "qhd,khd->hqk") * score_scale
            allowed = mask_for(own_segs, key_segs)[None]
            probs = jnp.exp(jnp.where(allowed, scores - log_sum[..., None], NEG_LARGE))
            grad_probs = product(grad_context_heads, value_block, "qhd,khd->hqk")
            grad_scores = (probs * (grad_probs - delta_heads[..., None])).astype(jnp.bfloat16)
            return grad_queries + product(grad_scores, key_block, "hqk,khd->qhd") * score_scale

        return lax.cond(active, query_live, keep_same, current)

    grad_queries = over_blocks(zero_heads, query_key_piece.shape[0], query_step_block)
    grad_joined = jnp.concatenate(
        [
            grad_queries.reshape(row_count, width),
            grad_keys.reshape(row_count, width),
            grad_values.reshape(row_count, width),
        ],
        axis=1,
    ).astype(jnp.bfloat16)
    grad_qkv_full = product(normed_low, grad_joined, "rd,re->de")
    grad_normed_in = product(grad_joined, qkv_full, "re,de->rd")
    _, in_back = jax.vjp(layer_norm, block_inputs, gain_in32)
    grad_from_in, grad_gain_in = in_back(grad_normed_in)
    grad_input = grad_residual + grad_from_in

    def own_half(full_array):
        share = full_array.shape[0] // fsdp_count
        return lax.dynamic_slice_in_dim(full_array, fsdp_at * share, share)

    accumulated_result = lax.psum(
        (
            grad_gain_in,
            grad_qkv_full,
            grad_out_full,
            grad_gain_mid,
            grad_router_full,
            grad_embed_full,
        ),
        ("ctx", "fsdp"),
    )
    grad_ln1 = own_half(accumulated_result[0])
    grad_qkv = own_half(accumulated_result[1])
    grad_output_weight = own_half(accumulated_result[2])
    grad_ln2 = own_half(accumulated_result[3])
    grad_router = own_half(accumulated_result[4])
    grad_embed = own_half(accumulated_result[5])
    expert_sums = (
        lax.psum_scatter(
            grad_up[None].astype(jnp.bfloat16), "fsdp", scatter_dimension=1, tiled=True
        ).astype(jnp.float32),
        lax.psum_scatter(
            grad_down[None].astype(jnp.bfloat16), "fsdp", scatter_dimension=1, tiled=True
        ).astype(jnp.float32),
    )
    grad_expert_up = expert_sums[0]
    grad_expert_down = expert_sums[1]
    return (
        result[None].astype(jnp.bfloat16),
        grad_input[None],
        grad_ln1,
        grad_qkv,
        grad_output_weight,
        grad_ln2,
        grad_router,
        grad_embed,
        grad_expert_up,
        grad_expert_down,
    )


def solution(mesh):
    return jax.shard_map(
        body,
        mesh=mesh,
        in_specs=(
            P("fsdp", "ctx", None),
            P("fsdp"),
            P("fsdp", None),
            P("fsdp", None),
            P("fsdp"),
            P("fsdp", None),
            P("fsdp", None),
            P("ctx", "fsdp", None),
            P("ctx", "fsdp", None),
            P("fsdp", "ctx"),
            P("fsdp", "ctx", None),
            P("fsdp", "ctx", None),
        ),
        out_specs=(
            P("fsdp", "ctx", None),
            P("fsdp", "ctx", None),
            P("fsdp"),
            P("fsdp", None),
            P("fsdp", None),
            P("fsdp"),
            P("fsdp", None),
            P("fsdp", None),
            P("ctx", "fsdp", None),
            P("ctx", "fsdp", None),
        ),
        check_vma=False,
    )
```

profile of v0, /device:TPU:0, one launch (start us, length us, event | category | flops | bytes accessed | tf_op | source)
XLA Modules:
  0.0 1100.4 jit_solution(7598676786807415787)
XLA Ops:
  16.4 45.3 %all-gather.12.cloned.1.call-done = bf16[768,2304]{1,0:T(8,128)(2,1)} async-done(((bf16[384,2304]{1,0:T(8,128)(2,1)}), bf16[768,2304]{1,0:T(8,128)(2,1)}) %all-gather.12.cloned.1.call-update) | async-done | bytes 3538960 | tf_op jit(solution)/shard_map/all_gather | solution.py:106
  73.7 22.7 %all-gather = s32[1,4096]{1,0:T(1,128)} all-gather(s32[1,256]{1,0:T(1,128)S(1)} %copy-done.24), channel_id=2, replica_groups=mesh['ctx'=16,'fsdp'=2] {'ctx'}, dimensions={1}, use_global_device_ids=true | all-gather | bytes 17408 | tf_op jit(solution)/shard_map/all_gather | solution.py:113
  97.4 30.6 %all-gather.14.cloned.1.call-done = bf16[4096,768]{1,0:T(8,128)(2,1)} async-done(((bf16[256,768]{1,0:T(8,128)(2,1)}), bf16[4096,768]{1,0:T(8,128)(2,1)}) %all-gather.14.cloned.1.call-update) | async-done | bytes 6291472 | tf_op jit(solution)/shard_map/all_gather | solution.py:131
  136.7 54.1 %all-gather.16.cloned.1.call-done = bf16[4096,768]{1,0:T(8,128)(2,1)} async-done(((bf16[256,768]{1,0:T(8,128)(2,1)}), bf16[4096,768]{1,0:T(8,128)(2,1)}) %all-gather.16.cloned.1.call-update) | async-done | bytes 6291472 | tf_op jit(solution)/shard_map/all_gather | solution.py:132
  199.6 96.1 %while.39 = (s32[]{:T(128)}, f32[12,256]{1,0:T(8,128)S(1)}, f32[12,256]{1,0:T(8,128)S(1)}, f32[12,256,64]{1,2,0:T(8,128)S(1)}, s32[8]{0:T(128)S(1)}, /*index=5*/...) while((s32[]{:T(128)}, f32[12,256]{1,0:T(8,128)S(1)}, ...), condition=%wide.region_7.8_spmd, body=%wide.region_2.7_spmd.sunk | while | flops 423630848 | bytes 26287524 | solution.py:65
  331.5 10.6 all-gather.22.cloned.1.call-done
  361.1 22.5 %all-to-all-done.1 = bf16[16,32,768]{2,1,0:T(8,128)(2,1)S(1)} async-done(((bf16[16,32,768]{2,1,0:T(8,128)(2,1)}), bf16[16,32,768]{2,1,0:T(8,128)(2,1)S(1)}, u32[]{:S(2)}, u32[]{:S(2)}) %all-to-all-start.1) | async-done | bytes 786464 | tf_op jit(solution)/shard_map/all_to_all | solution.py:202
  392.1 40.6 %all_to_all.20 = bf16[16,32,768]{2,1,0:T(8,128)(2,1)S(1)} all-to-all(bf16[16,32,768]{2,1,0:T(8,128)(2,1)S(1)} %bitcast.254), channel_id=1, replica_groups=mesh['ctx'=16,'fsdp'=2] {'ctx'}, dimensions={0} | all-to-all | bytes 1572864 | tf_op jit(solution)/shard_map/all_to_all | solution.py:211
  450.9 14.8 %all-to-all-done.3 = bf16[16,32,768]{2,1,0:T(8,128)(2,1)S(1)} async-done(((bf16[16,32,768]{2,1,0:T(8,128)(2,1)}), bf16[16,32,768]{2,1,0:T(8,128)(2,1)S(1)}, u32[]{:S(2)}, u32[]{:S(2)}) %all-to-all-start.3) | async-done | bytes 786464 | tf_op jit(solution)/shard_map/all_to_all | solution.py:223
  491.3 8.9 copy.59
  500.8 24.7 %all_gather.59 = f32[4096,12]{0,1:T(8,128)} all-gather(f32[256,12]{0,1:T(8,128)} %bitcast.56), channel_id=1, replica_groups=mesh['ctx'=16,'fsdp'=2] {'ctx'}, dimensions={0}, use_global_device_ids=true | all-gather | bytes 208896 | tf_op jit(solution)/shard_map/all_gather | solution.py:245
  529.1 146.0 %while.40 = (s32[]{:T(128)}, f32[256,12,64]{0,2,1:T(8,128)}, s32[8]{0:T(128)S(1)}, s32[4096]{0:T(1024)}, s32[]{:T(128)}, /*index=5*/s32[]{:T(128)}, bf16[4096,76...) while((s32[]{:T(128)}, f32[256,12,64]{0,2,1:T(8,128)}, ...), condition=%wide.region_31.32_spmd, body=%wide.region_28.31_spmd.sunk | while | flops 613941248 | bytes 20745632 | solution.py:65
  534.2 13.2 %conditional.7 = (f32[256,12,64]{0,2,1:T(8,128)}) conditional(s32[]{:T(128)} %convert_element_type.292, f32[256,12,64]{0,2,1:T(8,128)} %get-tuple-element.973, (s32[]{:T(128)}, bf16[4096,768]{0,1:T(8,128)(2,1)}, s32[512]{0:T(512)S(1)}, s32[1,256]{1,0:T(1,128)}, bf16[256,12,64]{0,2,1:T(8,128)(2,1)S(1)}, /*index=5*/f32[12,256]{1,0:T(8,128)}, ...), branch_computations={%region_29.29_spmd, %region_30.30_spmd} | conditional | flops 613941248 | bytes 20741194 | solution.py:307
  552.4 13.1 %conditional.7 = (f32[256,12,64]{0,2,1:T(8,128)}) conditional(s32[]{:T(128)} %convert_element_type.292, f32[256,12,64]{0,2,1:T(8,128)} %get-tuple-element.973, (s32[]{:T(128)}, bf16[4096,768]{0,1:T(8,128)(2,1)}, s32[512]{0:T(512)S(1)}, s32[1,256]{1,0:T(1,128)}, bf16[256,12,64]{0,2,1:T(8,128)(2,1)S(1)}, /*index=5*/f32[12,256]{1,0:T(8,128)}, ...), branch_computations={%region_29.29_spmd, %region_30.30_spmd} | conditional | flops 613941248 | bytes 20741194 | solution.py:307
  570.6 13.2 %conditional.7 = (f32[256,12,64]{0,2,1:T(8,128)}) conditional(s32[]{:T(128)} %convert_element_type.292, f32[256,12,64]{0,2,1:T(8,128)} %get-tuple-element.973, (s32[]{:T(128)}, bf16[4096,768]{0,1:T(8,128)(2,1)}, s32[512]{0:T(512)S(1)}, s32[1,256]{1,0:T(1,128)}, bf16[256,12,64]{0,2,1:T(8,128)(2,1)S(1)}, /*index=5*/f32[12,256]{1,0:T(8,128)}, ...), branch_computations={%region_29.29_spmd, %region_30.30_spmd} | conditional | flops 613941248 | bytes 20741194 | solution.py:307
  588.9 13.2 %conditional.7 = (f32[256,12,64]{0,2,1:T(8,128)}) conditional(s32[]{:T(128)} %convert_element_type.292, f32[256,12,64]{0,2,1:T(8,128)} %get-tuple-element.973, (s32[]{:T(128)}, bf16[4096,768]{0,1:T(8,128)(2,1)}, s32[512]{0:T(512)S(1)}, s32[1,256]{1,0:T(1,128)}, bf16[256,12,64]{0,2,1:T(8,128)(2,1)S(1)}, /*index=5*/f32[12,256]{1,0:T(8,128)}, ...), branch_computations={%region_29.29_spmd, %region_30.30_spmd} | conditional | flops 613941248 | bytes 20741194 | solution.py:307
  607.2 13.1 %conditional.7 = (f32[256,12,64]{0,2,1:T(8,128)}) conditional(s32[]{:T(128)} %convert_element_type.292, f32[256,12,64]{0,2,1:T(8,128)} %get-tuple-element.973, (s32[]{:T(128)}, bf16[4096,768]{0,1:T(8,128)(2,1)}, s32[512]{0:T(512)S(1)}, s32[1,256]{1,0:T(1,128)}, bf16[256,12,64]{0,2,1:T(8,128)(2,1)S(1)}, /*index=5*/f32[12,256]{1,0:T(8,128)}, ...), branch_computations={%region_29.29_spmd, %region_30.30_spmd} | conditional | flops 613941248 | bytes 20741194 | solution.py:307
  625.3 13.4 %conditional.7 = (f32[256,12,64]{0,2,1:T(8,128)}) conditional(s32[]{:T(128)} %convert_element_type.292, f32[256,12,64]{0,2,1:T(8,128)} %get-tuple-element.973, (s32[]{:T(128)}, bf16[4096,768]{0,1:T(8,128)(2,1)}, s32[512]{0:T(512)S(1)}, s32[1,256]{1,0:T(1,128)}, bf16[256,12,64]{0,2,1:T(8,128)(2,1)S(1)}, /*index=5*/f32[12,256]{1,0:T(8,128)}, ...), branch_computations={%region_29.29_spmd, %region_30.30_spmd} | conditional | flops 613941248 | bytes 20741194 | solution.py:307
  643.8 13.2 %conditional.7 = (f32[256,12,64]{0,2,1:T(8,128)}) conditional(s32[]{:T(128)} %convert_element_type.292, f32[256,12,64]{0,2,1:T(8,128)} %get-tuple-element.973, (s32[]{:T(128)}, bf16[4096,768]{0,1:T(8,128)(2,1)}, s32[512]{0:T(512)S(1)}, s32[1,256]{1,0:T(1,128)}, bf16[256,12,64]{0,2,1:T(8,128)(2,1)S(1)}, /*index=5*/f32[12,256]{1,0:T(8,128)}, ...), branch_computations={%region_29.29_spmd, %region_30.30_spmd} | conditional | flops 613941248 | bytes 20741194 | solution.py:307
  662.1 13.0 %conditional.7 = (f32[256,12,64]{0,2,1:T(8,128)}) conditional(s32[]{:T(128)} %convert_element_type.292, f32[256,12,64]{0,2,1:T(8,128)} %get-tuple-element.973, (s32[]{:T(128)}, bf16[4096,768]{0,1:T(8,128)(2,1)}, s32[512]{0:T(512)S(1)}, s32[1,256]{1,0:T(1,128)}, bf16[256,12,64]{0,2,1:T(8,128)(2,1)S(1)}, /*index=5*/f32[12,256]{1,0:T(8,128)}, ...), branch_computations={%region_29.29_spmd, %region_30.30_spmd} | conditional | flops 613941248 | bytes 20741194 | solution.py:307
  677.1 19.9 %all_gather.61 = f32[4096,12]{0,1:T(8,128)} all-gather(f32[256,12]{0,1:T(8,128)} %bitcast.272), channel_id=1, replica_groups=mesh['ctx'=16,'fsdp'=2] {'ctx'}, dimensions={0}, use_global_device_ids=true | all-gather | bytes 208896 | tf_op jit(solution)/shard_map/all_gather | solution.py:246
  708.6 183.1 %while.41 = (s32[]{:T(128)}, f32[256,12,64]{0,2,1:T(8,128)S(1)}, f32[256,12,64]{0,2,1:T(8,128)}, s32[8]{0:T(128)S(1)}, s32[4096]{0:T(1024)}, /*index=5*/s32[]{:T...) while((s32[]{:T(128)}, f32[256,12,64]{0,2,1:T(8,128)S(1)}, ...), condition=%wide.region_35.36_spmd, body=%wide.region_32.35_spmd.sunk | while | flops 821755904 | bytes 29670840 | solution.py:65
  713.7 17.8 %conditional.8 = ((f32[256,12,64]{0,2,1:T(8,128)S(1)}, f32[256,12,64]{0,2,1:T(8,128)})) conditional(s32[]{:T(128)} %convert_element_type.293, (f32[256,12,64]{0,2,1:T(8,128)S(1)}, f32[256,12,64]{0,2,1:T(8,128)}) %tuple.120, (s32[]{:T(128)}, bf16[4096,768]{0,1:T(8,128)(2,1)}, s32[1,256]{1,0:T(1,128)S(1)}, s32[512]{0:T(512)S(1)}, ...), branch_computations={%region_33.33_spmd, %region_34.34_spmd} | conditional | flops 821755904 | bytes 29666370 | solution.py:280
  736.6 17.8 %conditional.8 = ((f32[256,12,64]{0,2,1:T(8,128)S(1)}, f32[256,12,64]{0,2,1:T(8,128)})) conditional(s32[]{:T(128)} %convert_element_type.293, (f32[256,12,64]{0,2,1:T(8,128)S(1)}, f32[256,12,64]{0,2,1:T(8,128)}) %tuple.120, (s32[]{:T(128)}, bf16[4096,768]{0,1:T(8,128)(2,1)}, s32[1,256]{1,0:T(1,128)S(1)}, s32[512]{0:T(512)S(1)}, ...), branch_computations={%region_33.33_spmd, %region_34.34_spmd} | conditional | flops 821755904 | bytes 29666370 | solution.py:280
  759.5 17.8 %conditional.8 = ((f32[256,12,64]{0,2,1:T(8,128)S(1)}, f32[256,12,64]{0,2,1:T(8,128)})) conditional(s32[]{:T(128)} %convert_element_type.293, (f32[256,12,64]{0,2,1:T(8,128)S(1)}, f32[256,12,64]{0,2,1:T(8,128)}) %tuple.120, (s32[]{:T(128)}, bf16[4096,768]{0,1:T(8,128)(2,1)}, s32[1,256]{1,0:T(1,128)S(1)}, s32[512]{0:T(512)S(1)}, ...), branch_computations={%region_33.33_spmd, %region_34.34_spmd} | conditional | flops 821755904 | bytes 29666370 | solution.py:280
  782.4 17.8 %conditional.8 = ((f32[256,12,64]{0,2,1:T(8,128)S(1)}, f32[256,12,64]{0,2,1:T(8,128)})) conditional(s32[]{:T(128)} %convert_element_type.293, (f32[256,12,64]{0,2,1:T(8,128)S(1)}, f32[256,12,64]{0,2,1:T(8,128)}) %tuple.120, (s32[]{:T(128)}, bf16[4096,768]{0,1:T(8,128)(2,1)}, s32[1,256]{1,0:T(1,128)S(1)}, s32[512]{0:T(512)S(1)}, ...), branch_computations={%region_33.33_spmd, %region_34.34_spmd} | conditional | flops 821755904 | bytes 29666370 | solution.py:280
  805.3 17.8 %conditional.8 = ((f32[256,12,64]{0,2,1:T(8,128)S(1)}, f32[256,12,64]{0,2,1:T(8,128)})) conditional(s32[]{:T(128)} %convert_element_type.293, (f32[256,12,64]{0,2,1:T(8,128)S(1)}, f32[256,12,64]{0,2,1:T(8,128)}) %tuple.120, (s32[]{:T(128)}, bf16[4096,768]{0,1:T(8,128)(2,1)}, s32[1,256]{1,0:T(1,128)S(1)}, s32[512]{0:T(512)S(1)}, ...), branch_computations={%region_33.33_spmd, %region_34.34_spmd} | conditional | flops 821755904 | bytes 29666370 | solution.py:280
  828.2 17.8 %conditional.8 = ((f32[256,12,64]{0,2,1:T(8,128)S(1)}, f32[256,12,64]{0,2,1:T(8,128)})) conditional(s32[]{:T(128)} %convert_element_type.293, (f32[256,12,64]{0,2,1:T(8,128)S(1)}, f32[256,12,64]{0,2,1:T(8,128)}) %tuple.120, (s32[]{:T(128)}, bf16[4096,768]{0,1:T(8,128)(2,1)}, s32[1,256]{1,0:T(1,128)S(1)}, s32[512]{0:T(512)S(1)}, ...), branch_computations={%region_33.33_spmd, %region_34.34_spmd} | conditional | flops 821755904 | bytes 29666370 | solution.py:280
  851.1 17.8 %conditional.8 = ((f32[256,12,64]{0,2,1:T(8,128)S(1)}, f32[256,12,64]{0,2,1:T(8,128)})) conditional(s32[]{:T(128)} %convert_element_type.293, (f32[256,12,64]{0,2,1:T(8,128)S(1)}, f32[256,12,64]{0,2,1:T(8,128)}) %tuple.120, (s32[]{:T(128)}, bf16[4096,768]{0,1:T(8,128)(2,1)}, s32[1,256]{1,0:T(1,128)S(1)}, s32[512]{0:T(512)S(1)}, ...), branch_computations={%region_33.33_spmd, %region_34.34_spmd} | conditional | flops 821755904 | bytes 29666370 | solution.py:280
  874.0 17.7 %conditional.8 = ((f32[256,12,64]{0,2,1:T(8,128)S(1)}, f32[256,12,64]{0,2,1:T(8,128)})) conditional(s32[]{:T(128)} %convert_element_type.293, (f32[256,12,64]{0,2,1:T(8,128)S(1)}, f32[256,12,64]{0,2,1:T(8,128)}) %tuple.120, (s32[]{:T(128)}, bf16[4096,768]{0,1:T(8,128)(2,1)}, s32[1,256]{1,0:T(1,128)S(1)}, s32[512]{0:T(512)S(1)}, ...), branch_computations={%region_33.33_spmd, %region_34.34_spmd} | conditional | flops 821755904 | bytes 29666370 | solution.py:280
  911.5 39.2 %all-reduce = (f32[768]{0:T(1024)S(1)}, f32[768]{0:T(1024)S(1)}, f32[768,16]{0,1:T(8,128)S(1)}, f32[16,16]{1,0:T(8,128)S(1)}) all-reduce(f32[768]{0:T(1024)S(1)} %get-tuple-element.448, f32[768]{0:T(1024)} %get-tuple-element.446, f32[768,16]{0,1:T(8,128)} %fusion.128, ...), channel_id=1, replica_groups=mesh['ctx'=16,'fsdp'=2] {'ctx','fsdp'}, use_global_device_ids=true, to_apply=%region_39.40 | all-reduce | flops 14080 | bytes 112640 | tf_op jit(solution)/shard_map/psum | solution.py:328
  955.2 133.2 %all-reduce.4.cloned.1.call-done = (f32[768,2304]{1,0:T(8,128)}, f32[768,768]{1,0:T(8,128)}) async-done(((f32[768,2304]{1,0:T(8,128)}, f32[768,768]{1,0:T(8,128)}), (f32[768,2304]{1,0:T(8,128)}, f32[768,768]{1,0:T(8,128)})) %all-reduce.4.cloned.1.call-update) | async-done | bytes 9437200 | tf_op jit(solution)/shard_map/psum | solution.py:328
  (523 shorter events, 597.1 us)
Async XLA Ops:
  7.2 54.5 %all-gather.12.cloned.1.call-start = ((), (), s32[]{:S(2)}) async-start(), calls=%async_computation.6 | async-start | bytes 5308416 | tf_op jit(solution)/shard_map/all_gather | solution.py:106
  7.9 120.1 %all-gather.14.cloned.1.call-start = ((), (), s32[]{:S(2)}) async-start(), calls=%async_computation.7 | async-start | bytes 6684672 | tf_op jit(solution)/shard_map/all_gather | solution.py:131
  13.9 53.9 %copy-start.27 = (f32[768]{0:T(1024)}, f32[768]{0:T(1024)S(1)}, u32[]{:S(2)}) copy-start(f32[768]{0:T(1024)S(1)} %reshape.422) | copy-start | bytes 9220
  15.1 53.4 %copy-start.38 = (f32[256]{0:T(256)}, f32[256]{0:T(256)S(1)}, u32[]{:S(2)}) copy-start(f32[256]{0:T(256)S(1)} %broadcast_multiply_fusion.1) | copy-start | bytes 3076
  16.3 52.1 %copy-start.50 = (f32[256]{0:T(256)}, f32[256]{0:T(256)S(1)}, u32[]{:S(2)}) copy-start(f32[256]{0:T(256)S(1)} %fusion.81) | copy-start | bytes 3076
  16.3 52.1 %copy-start.43 = (f32[256]{0:T(256)}, f32[256]{0:T(256)S(1)}, u32[]{:S(2)}) copy-start(f32[256]{0:T(256)S(1)} %fusion.119) | copy-start | bytes 3076
  16.3 52.2 %copy-start.41 = (s32[1,256,1]{1,2,0:T(1,128)S(1)}, s32[1,256,1]{1,2,0:T(1,128)}, u32[]{:S(2)}) copy-start(s32[1,256,1]{1,2,0:T(1,128)} %param.34) | copy-start | bytes 3076
  16.3 53.0 %copy-start.66 = (bf16[384]{0:T(512)(128)(2,1)S(1)}, bf16[384]{0:T(512)(128)(2,1)}, u32[]{:S(2)}) copy-start(bf16[384]{0:T(512)(128)(2,1)} %param.28) | copy-start | bytes 2308
  16.4 57.4 %copy-start.24 = (s32[1,256]{1,0:T(1,128)S(1)}, s32[1,256]{1,0:T(1,128)}, u32[]{:S(2)}) copy-start(s32[1,256]{1,0:T(1,128)} %param.33) | copy-start | bytes 3076
  65.9 124.9 %all-gather.16.cloned.1.call-start = ((), (), s32[]{:S(2)}) async-start(), calls=%async_computation.8 | async-start | bytes 6684672 | tf_op jit(solution)/shard_map/all_gather | solution.py:132
  66.7 229.2 %all-gather.18.cloned.1.call-start = ((), (), s32[]{:S(2)}) async-start(), calls=%async_computation.9 | async-start | bytes 1769472 | tf_op jit(solution)/shard_map/all_gather | solution.py:107
  67.2 249.2 %all-gather.20.cloned.1.call-start = ((), (), s32[]{:S(2)}) async-start(), calls=%async_computation.10 | async-start | bytes 7077888 | tf_op jit(solution)/shard_map/all_gather | solution.py:111
  67.8 274.3 %all-gather.22.cloned.1.call-start = ((), (), s32[]{:S(2)}) async-start(), calls=%async_computation.11 | async-start | bytes 7077888 | tf_op jit(solution)/shard_map/all_gather | solution.py:198
  68.5 422.9 %all-gather.24.cloned.1.call-start = ((), (), s32[]{:S(2)}) async-start(), calls=%async_computation.12 | async-start | bytes 6684672 | tf_op jit(solution)/shard_map/all_gather | solution.py:249
  73.7 224.8 %copy-start.33 = (f32[768]{0:T(1024)}, f32[768]{0:T(1024)S(1)}, u32[]{:S(2)}) copy-start(f32[768]{0:T(1024)S(1)} %reshape.423) | copy-start | bytes 9220
  97.2 201.3 %copy-start.60 = (s32[256,1]{0,1:T(1,128)}, s32[256,1]{0,1:T(1,128)S(1)}, u32[]{:S(2)}) copy-start(s32[256,1]{0,1:T(1,128)S(1)} %compare_select_fusion) | copy-start | bytes 3076
  199.6 96.8 %copy-start = (bf16[1,256,768]{2,1,0:T(8,128)(2,1)S(1)}, bf16[1,256,768]{2,1,0:T(8,128)(2,1)}, u32[]{:S(2)}) copy-start(bf16[1,256,768]{2,1,0:T(8,128)(2,1)} %param.24) | copy-start | bytes 1179652
  301.2 22.4 %all-to-all-start = ((bf16[16,32,768]{2,1,0:T(8,128)(2,1)}), bf16[16,32,768]{2,1,0:T(8,128)(2,1)S(1)}, u32[]{:S(2)}, u32[]{:S(2)}) async-start(bf16[16,32,768]{2,1,0:T(8,128)(2,1)} %bitcast.39), calls=%async_computation | async-start | bytes 1572864 | tf_op jit(solution)/shard_map/all_to_all | solution.py:190
  348.9 34.6 %all-to-all-start.1 = ((bf16[16,32,768]{2,1,0:T(8,128)(2,1)}), bf16[16,32,768]{2,1,0:T(8,128)(2,1)S(1)}, u32[]{:S(2)}, u32[]{:S(2)}) async-start(bf16[16,32,768]{2,1,0:T(8,128)(2,1)} %bitcast.265), calls=%async_computation.1 | async-start | bytes 1572864 | tf_op jit(solution)/shard_map/all_to_all | solution.py:202
  392.1 47.6 %slice-start = ((s8[4718592]{0:T(1024)(128)(4,1)}), s8[4194304]{0:T(1024)(128)(4,1)S(1)}, s32[]{:S(2)}) async-start(s8[4718592]{0:T(1024)(128)(4,1)} %bitcast.283), calls=%async_computation.17 | async-start | bytes 8388608
  443.3 22.4 %all-to-all-start.3 = ((bf16[16,32,768]{2,1,0:T(8,128)(2,1)}), bf16[16,32,768]{2,1,0:T(8,128)(2,1)S(1)}, u32[]{:S(2)}, u32[]{:S(2)}) async-start(bf16[16,32,768]{2,1,0:T(8,128)(2,1)} %bitcast.266), calls=%async_computation.3 | async-start | bytes 1572864 | tf_op jit(solution)/shard_map/all_to_all | solution.py:223
  447.0 251.9 %all-gather.26.cloned.1.call-start = ((), (), s32[]{:S(2)}) async-start(), calls=%async_computation.13 | async-start | bytes 6684672 | tf_op jit(solution)/shard_map/all_gather | solution.py:250
  475.8 424.5 %reduce-scatter.5.cloned.1.call-start = ((), (), s32[]{:S(2)}) async-start(), calls=%async_computation.15 | async-start | bytes 7077888 | tf_op jit(solution)/shard_map/reduce_scatter | solution.py:349
  482.8 422.3 %reduce-scatter.3.cloned.1.call-start = ((), (), s32[]{:S(2)}) async-start(), calls=%async_computation.14 | async-start | bytes 7077888 | tf_op jit(solution)/shard_map/reduce_scatter | solution.py:346
  490.1 598.3 %all-reduce.4.cloned.1.call-start = ((), (), s32[]{:S(2)}) async-start(), calls=%async_computation.16 | async-start | bytes 18874368 | tf_op jit(solution)/shard_map/psum | solution.py:328
  529.1 167.9 %copy-start.10 = (bf16[256,12,64]{0,2,1:T(8,128)(2,1)S(1)}, bf16[256,12,64]{0,2,1:T(8,128)(2,1)}, u32[]{:S(2)}) copy-start(bf16[256,12,64]{0,2,1:T(8,128)(2,1)} %copy-done.9) | copy-start | bytes 1179652
  529.1 167.9 %copy-start.14 = (bf16[256,768]{1,0:T(8,128)(2,1)S(1)}, bf16[256,768]{1,0:T(8,128)(2,1)}, u32[]{:S(2)}) copy-start(bf16[256,768]{1,0:T(8,128)(2,1)} %copy-done.13) | copy-start | bytes 1179652
  708.6 184.5 %copy-start.28 = (f32[768]{0:T(1024)S(1)}, f32[768]{0:T(1024)}, u32[]{:S(2)}) copy-start(f32[768]{0:T(1024)} %copy-done.27) | copy-start | bytes 9220
  708.6 184.5 %copy-start.39 = (f32[256]{0:T(256)S(1)}, f32[256]{0:T(256)}, u32[]{:S(2)}) copy-start(f32[256]{0:T(256)} %copy-done.38) | copy-start | bytes 3076
  708.6 184.5 %copy-start.44 = (f32[256]{0:T(256)S(1)}, f32[256]{0:T(256)}, u32[]{:S(2)}) copy-start(f32[256]{0:T(256)} %copy-done.43) | copy-start | bytes 3076
  909.8 43.5 %copy-start.2 = (f32[256,768]{1,0:T(8,128)S(1)}, f32[256,768]{1,0:T(8,128)}, u32[]{:S(2)}) copy-start(f32[256,768]{1,0:T(8,128)} %copy-done.1) | copy-start | bytes 2359300
  909.8 43.5 %copy-start.4 = (bf16[1,256,768]{2,1,0:T(8,128)(2,1)S(1)}, bf16[1,256,768]{2,1,0:T(8,128)(2,1)}, u32[]{:S(2)}) copy-start(bf16[1,256,768]{2,1,0:T(8,128)(2,1)} %param.35) | copy-start | bytes 1179652
  (64 other events, 348.7 us)
Sparse Core Ops, SparseCore 0:
  9.6 52.0 all-gather.11
  66.1 61.9 all-gather.13
  130.3 60.4 all-gather.15
  192.2 21.3 all-gather.17
  215.0 62.6 all-gather.19
  279.1 62.9 all-gather.21
  344.4 89.0 all-gather.23
  475.9 64.4 all-gather.25
  543.3 58.7 reduce-scatter.4
  604.9 59.9 reduce-scatter.2
  898.6 189.7 all-reduce.3
where the time goes:
time: 1110 us; the launch traced here: 1100 us
  waiting for transfers between devices  321 us (29%)
  matrix products  282 us (25%)
  blocking collectives  166 us (15%)
  local copies, waits for them, and re-layouts  164 us (15%)
  loops' own time  76.6 us (7%)
  other arithmetic  60.8 us (5%)
  between operations  15 us (1%)
  starting transfers between devices  13.9 us (1%)
    dot_general x64, matrix products, product(): return jnp.einsum(pattern, left, right, preferred_element_type=jnp.float32)  255 us
    psum x1, waiting for transfers between devices, body(): lax.psum((grad_gain_in, grad_qkv_full, grad_out_full, grad_gain_mid, grad...  133 us
    another operation x3, loops' own time, over_blocks(): lax.scan(advance, state, jnp.arange(piece_rows // block_rows, dtype=jnp.i...  75.3 us
    all_gather x1, waiting for transfers between devices, body(): value_piece = lax.all_gather(value_rows, 'ctx', axis=0, tiled=True)  54.1 us
    all_gather x1, waiting for transfers between devices, body(): lax.all_gather(asker_lookup_content_maps, 'fsdp', axis=0, tiled=True)  45.3 us
    all_to_all x1, blocking collectives, body(): lax.all_to_all(grad_send.reshape(ctx_count, capacity, width), 'ctx', spli...  40.6 us
    psum x1, blocking collectives, body(): lax.psum((grad_gain_in, grad_qkv_full, grad_out_full, grad_gain_mid, grad...  39.2 us
    while x4, local copies, waits for them, and re-layouts, over_blocks(): lax.scan(advance, state, jnp.arange(piece_rows // block_rows, dtype=jnp.i...  34.9 us
  transfers between devices with their start and end apart: 14, of which 8 were waited for; matrix products, arithmetic and copies ran while one was open for 45% of the time, Pallas kernels for 0%

commit v1 on v0

v1 whole, which is shorter than its diff:
```python
import functools
import math

import jax
import jax.numpy as jnp
from jax import lax
from jax.experimental import pallas as pl
from jax.experimental.pallas import tpu as pltpu
from jax.sharding import Mesh, PartitionSpec as P

HD = 64
DOCS = 8
AUX = 16
GROUPS = 4
EPSILON = 1e-05
FLOOR = 0.5
ROUTER_HEAT = 0.5
HIGHEST = lax.Precision.HIGHEST
ROOT_HALF = 0.7071067811865476
ROOT_TWO_PI = 2.5066282746310002
NEG_LARGE = -1e30
LOG2E = 1.4426950408889634
VMEM_BYTES = 48 * 1024 * 1024
BF16 = jnp.bfloat16
F32 = jnp.float32


def dot32(left, right, dims):
    return lax.dot_general(left, right, (dims, ((), ())), preferred_element_type=F32)


def forward_kernel(scale2, last, q_ref, oh_ref, k_ref, v_ref, mk_ref, *rest):
    if last:
        top_in, acc_in, out_ref, lse_ref, top_sc, acc_sc = rest
    else:
        top_out, acc_out, top_sc, acc_sc = rest
    step = pl.program_id(1)
    width = k_ref.shape[-1]
    block = min(512, width)
    pad = jnp.zeros((128 - HD - AUX, q_ref.shape[-1]), BF16)
    query = jnp.concatenate([q_ref[...], oh_ref[...], pad], axis=0)

    @pl.when(step == 0)
    def _():
        if last:
            top_sc[...] = top_in[0]
            acc_sc[...] = acc_in[0]
        else:
            top_sc[...] = jnp.full_like(top_sc, NEG_LARGE)
            acc_sc[...] = jnp.zeros_like(acc_sc)

    top, acc = top_sc[...], acc_sc[...]
    for at in range(0, width, block):
        cut = slice(at, at + block)
        aux = mk_ref[0, :, cut]
        keys = jnp.concatenate([k_ref[0, :, cut], aux, pad[:, :block]], axis=0).T
        scores = jnp.dot(keys, query, preferred_element_type=F32)
        new_top = jnp.maximum(top, jnp.max(scores, axis=0, keepdims=True))
        probs = jnp.exp2((scores - new_top) * scale2).astype(BF16)
        decay = jnp.exp2((top - new_top) * scale2)
        values = jnp.concatenate([v_ref[0, :, cut], aux], axis=0)
        acc = acc * decay + jnp.dot(values, probs, preferred_element_type=F32)
        top = new_top
    top_sc[...], acc_sc[...] = top, acc

    @pl.when(step == pl.num_programs(1) - 1)
    def _():
        if last:
            total = acc[HD + DOCS : HD + DOCS + 1]
            out_ref[0] = acc[:HD] / total
            lse_ref[0] = top + jnp.log2(total) / scale2
        else:
            top_out[0] = top
            acc_out[0] = acc


def attend(query_t, onehot, pieces, carry, scale2, heads):
    count, _, width = pieces.shape
    rows = query_t.shape[1]
    last = carry is not None
    q_spec = pl.BlockSpec((HD, rows), lambda h, j: (h, 0))
    top_spec = pl.BlockSpec((1, 1, rows), lambda h, j: (h, 0, 0))
    acc_spec = pl.BlockSpec((1, HD + AUX, rows), lambda h, j: (h, 0, 0))
    in_specs = [
        q_spec,
        pl.BlockSpec((AUX, rows), lambda h, j: (0, 0)),
        pl.BlockSpec((1, HD, width), lambda h, j: (j, h, 0)),
        pl.BlockSpec((1, HD, width), lambda h, j: (j, heads + h, 0)),
        pl.BlockSpec((1, AUX, width), lambda h, j: (j, 2 * heads * HD // AUX, 0)),
    ]
    top_shape = jax.ShapeDtypeStruct((heads, 1, rows), F32)
    if last:
        in_specs += [top_spec, acc_spec]
        out_specs = [pl.BlockSpec((1, HD, rows), lambda h, j: (h, 0, 0)), top_spec]
        out_shape = [jax.ShapeDtypeStruct((heads, HD, rows), F32), top_shape]
    else:
        out_specs = [top_spec, acc_spec]
        out_shape = [top_shape, jax.ShapeDtypeStruct((heads, HD + AUX, rows), F32)]
    pairs = heads * rows * count * width
    return pl.pallas_call(
        functools.partial(forward_kernel, scale2, last),
        grid=(heads, count),
        in_specs=in_specs,
        out_specs=out_specs,
        out_shape=out_shape,
        scratch_shapes=[pltpu.VMEM((1, rows), F32), pltpu.VMEM((HD + AUX, rows), F32)],
        compiler_params=pltpu.CompilerParams(vmem_limit_bytes=VMEM_BYTES),
        cost_estimate=pl.CostEstimate(
            flops=16 * pairs * HD, bytes_accessed=4 * count * width * HD * heads, transcendentals=pairs
        ),
    )(query_t, onehot, pieces, pieces, pieces, *(carry or ()))


def split3(value):
    high = value.astype(BF16)
    rest = value - high.astype(F32)
    mid = rest.astype(BF16)
    return high, mid, (rest - mid.astype(F32)).astype(BF16)


def backward_kernel(
    scale2, q_ref, oh_ref, g_ref, o_ref, lse_ref, k_ref, v_ref, mk_ref, dq_ref, dkv_ref, qa_sc, ga_sc, nat_sc, dq_sc
):
    step = pl.program_id(0)
    width = k_ref.shape[-1]
    block = min(256, width)
    rows = q_ref.shape[-1]
    pad = jnp.zeros((128 - HD - AUX, rows), BF16)

    @pl.when(step == 0)
    def _():
        query, grad = q_ref[...], g_ref[...]
        delta = jnp.sum(grad.astype(F32) * o_ref[0], axis=0, keepdims=True)
        place = lax.broadcasted_iota(jnp.int32, (AUX, rows), 0)

        def aux_rows(start, value):
            out = start
            for at, piece in enumerate(split3(-value)):
                out = jnp.where(place == DOCS + at, piece.astype(F32), out)
            return out.astype(BF16)

        qa_sc[...] = jnp.concatenate([query, aux_rows(oh_ref[...].astype(F32), lse_ref[0]), pad], axis=0)
        ga_sc[...] = jnp.concatenate([grad, aux_rows(jnp.zeros((AUX, rows), F32), delta), pad], axis=0)
        nat_sc[...] = jnp.concatenate([grad, query], axis=0).T
        dq_sc[...] = jnp.zeros_like(dq_sc)

    natural = nat_sc[...]
    for at in range(0, width, block):
        cut = slice(at, at + block)
        aux = mk_ref[0, :, cut]
        keys_t = k_ref[0, :, cut]
        keys = jnp.concatenate([keys_t, aux, pad[:, :block]], axis=0).T
        values = jnp.concatenate([v_ref[0, :, cut], aux, pad[:, :block]], axis=0).T
        probs = jnp.exp2(jnp.dot(keys, qa_sc[...], preferred_element_type=F32) * scale2)
        slopes = jnp.dot(values, ga_sc[...], preferred_element_type=F32)
        grad_scores = (probs * slopes).astype(BF16)
        from_probs = jnp.dot(probs.astype(BF16), natural, preferred_element_type=F32)
        from_scores = jnp.dot(grad_scores, natural, preferred_element_type=F32) * (1.0 / math.sqrt(HD))
        lane = lax.broadcasted_iota(jnp.int32, from_probs.shape, 1)
        dkv_ref[0, :, cut] = jnp.where(lane < HD, from_probs, from_scores).T.astype(BF16)
        dq_sc[...] += jnp.dot(keys_t, grad_scores, preferred_element_type=F32)

    @pl.when(step == pl.num_programs(0) - 1)
    def _():
        dq_ref[...] = (dq_sc[...] * (1.0 / math.sqrt(HD))).astype(BF16)


def attend_back(head, query_t, onehot, grad_t, out_heads, lse, pieces, scale2, heads):
    count, _, width = pieces.shape
    rows = query_t.shape[1]
    pairs = rows * count * width
    return pl.pallas_call(
        functools.partial(backward_kernel, scale2),
        grid=(count,),
        in_specs=[
            pl.BlockSpec((HD, rows), lambda j: (head, 0)),
            pl.BlockSpec((AUX, rows), lambda j: (0, 0)),
            pl.BlockSpec((HD, rows), lambda j: (head, 0)),
            pl.BlockSpec((1, HD, rows), lambda j: (head, 0, 0)),
            pl.BlockSpec((1, 1, rows), lambda j: (head, 0, 0)),
            pl.BlockSpec((1, HD, width), lambda j: (j, head, 0)),
            pl.BlockSpec((1, HD, width), lambda j: (j, heads + head, 0)),
            pl.BlockSpec((1, AUX, width), lambda j: (j, 2 * heads * HD // AUX, 0)),
        ],
        out_specs=[
            pl.BlockSpec((HD, rows), lambda j: (0, 0)),
            pl.BlockSpec((1, 2 * HD, width), lambda j: (j, 0, 0)),
        ],
        out_shape=[
            jax.ShapeDtypeStruct((HD, rows), BF16),
            jax.ShapeDtypeStruct((count, 2 * HD, width), BF16),
        ],
        scratch_shapes=[
            pltpu.VMEM((128, rows), BF16),
            pltpu.VMEM((128, rows), BF16),
            pltpu.VMEM((rows, 128), BF16),
            pltpu.VMEM((HD, rows), F32),
        ],
        compiler_params=pltpu.CompilerParams(vmem_limit_bytes=VMEM_BYTES),
        cost_estimate=pl.CostEstimate(
            flops=40 * pairs * HD, bytes_accessed=8 * count * width * HD, transcendentals=pairs
        ),
    )(query_t, onehot, grad_t, out_heads, lse, pieces, pieces, pieces)


def norm_parts(values):
    center = values - jnp.mean(values, axis=-1, keepdims=True)
    scale = lax.rsqrt(jnp.mean(center * center, axis=-1, keepdims=True) + EPSILON)
    return center * scale, scale


def norm_back(unit, scale, scaled_grad):
    along = jnp.mean(scaled_grad * unit, axis=-1, keepdims=True)
    return scale * (scaled_grad - jnp.mean(scaled_grad, axis=-1, keepdims=True) - unit * along)


def unit_of(vectors, axis):
    size = jnp.sqrt(jnp.sum(vectors * vectors, axis=axis, keepdims=True))
    share = jnp.where(size > FLOOR, 1.0, jnp.where(size == FLOOR, 0.5, 0.0))
    inverse = 1.0 / jnp.maximum(size, FLOOR)
    return vectors * inverse, inverse, share


def unit_back(unit, inverse, share, grad, axis):
    return inverse * (grad - share * unit * jnp.sum(unit * grad, axis=axis, keepdims=True))


def shift(value, axis, size, by):
    return lax.ppermute(value, axis, [(at, (at + by) % size) for at in range(size)])


def flip(value, axis, size, bit):
    return lax.ppermute(value, axis, [(at, at ^ bit) for at in range(size)])


def after(value, *others):
    return lax.optimization_barrier((value, *others))[0]


def line_gather(value, axis, size):
    upward, downward, from_low, from_high = value, value, [], []
    for hop in range(size - 1):
        upward = lax.ppermute(upward, axis, [(at, at + 1) for at in range(hop, size - 1)])
        downward = lax.ppermute(downward, axis, [(at, at - 1) for at in range(size - 1 - hop, 0, -1)])
        from_low.append(upward)
        from_high.append(downward)
    return [value] + [from_low[k] + from_high[size - 2 - k] for k in range(size - 1)]


def roll_blocks(blocks, start):
    return lax.dynamic_slice_in_dim(jnp.concatenate([blocks, blocks], axis=0), start, blocks.shape[0], 0)


def pair_order(own, other, at):
    return jnp.where(at == 0, jnp.concatenate([own, other], 0), jnp.concatenate([other, own], 0))


def body(
    ctx_count,
    fsdp_count,
    incoming_sequence,
    mixer_scaling_factor,
    asker_lookup_content_maps,
    mixer_final_map,
    specialist_scaling_factor,
    dispatch_space_map,
    specialist_dispatch_vectors,
    specialist_widen_weights_pair,
    specialist_shrink_weights_pair,
    document_labels,
    piece_specialist_choice,
    result_cotangent_array,
):
    row_count = incoming_sequence.shape[1]
    width = incoming_sequence.shape[2]
    head_count = width // HD
    heads = head_count // GROUPS
    group_width = heads * HD
    ring = ctx_count // GROUPS
    bits = ring.bit_length() - 1
    scale2 = LOG2E / math.sqrt(HD)
    z_at = lax.axis_index("z")
    r_at = lax.axis_index("r")
    f_at = lax.axis_index("fsdp")
    core = r_at & 1
    expert_at = z_at * ring + r_at
    share = width // fsdp_count
    capacity = max(2, 2 * row_count // ctx_count)
    slots = ctx_count * capacity

    def swap(value):
        return flip(value, "fsdp", fsdp_count, 1)

    def across(value, bit):
        return flip(value, "r", ring, bit)

    def exchange_slots(rows):
        return lax.all_to_all(
            rows.reshape(ctx_count, capacity, -1), ("z", "r"), split_axis=0, concat_axis=0, tiled=True
        ).reshape(slots, -1)

    def other_half(piece):
        part = piece.shape[0] // 2
        got = swap(lax.dynamic_slice_in_dim(piece, core * part, part, 0))
        return pair_order(got, across(got, 1), core)

    x_own = incoming_sequence[0]
    label_rows = jnp.zeros((16, width), BF16).at[0, :row_count].set(document_labels[0].astype(BF16))
    blocks = line_gather(jnp.concatenate([x_own, label_rows], axis=0), "z", GROUPS)
    x_all = jnp.concatenate([piece[:row_count] for piece in blocks], axis=0)
    labels = jnp.concatenate([piece[row_count, :row_count] for piece in blocks], axis=0)

    gains_own = jnp.stack([mixer_scaling_factor, specialist_scaling_factor])
    gains_other = swap(gains_own)
    gains = jnp.where(
        f_at == 0,
        jnp.concatenate([gains_own, gains_other], 1),
        jnp.concatenate([gains_other, gains_own], 1),
    ).astype(F32)
    gain_in, gain_mid = gains[0], gains[1]

    maps = asker_lookup_content_maps.reshape(share, 3, GROUPS, group_width)
    maps_own = lax.dynamic_index_in_dim(maps, z_at, 2, keepdims=False).reshape(share, 3 * group_width)
    maps_other = swap(maps_own)
    maps_group = pair_order(maps_own, maps_other, f_at)
    router = pair_order(dispatch_space_map, swap(dispatch_space_map), f_at)
    embed = pair_order(specialist_dispatch_vectors, swap(specialist_dispatch_vectors), f_at).astype(F32)
    final_other = other_half(after(mixer_final_map, maps_other))
    final_map = pair_order(mixer_final_map, final_other, f_at)
    widen = specialist_widen_weights_pair[0]
    shrink_own = specialist_shrink_weights_pair[0]
    half_ff = shrink_own.shape[0]

    def swap_columns(value):
        return jnp.where(
            f_at == 0, value, jnp.concatenate([value[:, half_ff:], value[:, :half_ff]], axis=1)
        )

    widen_own = swap_columns(widen)
    widen_sent = jnp.concatenate([widen_own[:, half_ff:], widen_own[:, :half_ff]], axis=1)
    widen_other = swap(after(widen_sent, final_other))
    shrink_other = swap(after(shrink_own, widen_other))
    maps_rest = other_half(after(asker_lookup_content_maps, shrink_other))
    maps_full = pair_order(asker_lookup_content_maps, maps_rest, f_at)

    unit_all, _ = norm_parts(x_all.astype(F32))
    normed_low = (unit_all * gain_in).astype(BF16)
    joined_t = dot32(maps_group, normed_low, (((0,), (1,)))).astype(BF16)
    query_t = joined_t[:group_width]
    rows = x_all.shape[0]
    aux_at = jnp.arange(AUX, dtype=jnp.int32)[:, None]
    same = labels.astype(jnp.int32)[None, :] == aux_at
    onehot = same.astype(BF16)
    key_aux = jnp.where(
        aux_at < DOCS, jnp.where(same, 0.0, NEG_LARGE), jnp.where(aux_at < DOCS + 3, 1.0, 0.0)
    ).astype(BF16)
    own_piece = jnp.concatenate([joined_t[group_width:], key_aux], axis=0)[None]
    near = jnp.concatenate([own_piece, across(own_piece, 1)], axis=0)
    evens = own_piece
    for bit in range(bits - 1, 0, -1):
        got = across(evens, 1 << bit)
        evens = jnp.stack([evens, got], axis=1).reshape(-1, *own_piece.shape[1:]) if bit == 1 else jnp.concatenate([evens, got], axis=0)
    far = jnp.stack([evens[1:], across(evens[1:], 1)], axis=1).reshape(-1, *own_piece.shape[1:])

    carry = attend(query_t, onehot, near, None, scale2, heads)
    out_heads, lse = attend(query_t, onehot, far, carry, scale2, heads)
    out_low = out_heads.astype(BF16).reshape(group_width, GROUPS, row_count)
    context_parts = [
        out_low[:, k] if k == 0 else shift(out_low[:, k], "z", GROUPS, -k) for k in range(GROUPS)
    ]
    context_t = roll_blocks(jnp.stack(context_parts), (GROUPS - z_at) % GROUPS).reshape(width, row_count)

    x32 = x_own.astype(F32)
    residual = x32 + dot32(context_t, final_map, (((0,), (0,))))
    unit_mid, scale_mid = norm_parts(residual)
    mid_low = (unit_mid * gain_mid).astype(BF16)
    picked = piece_specialist_choice[0, :, 0]
    hits = (picked[:, None] == jnp.arange(ctx_count, dtype=jnp.int32)[None, :]).astype(jnp.int32)
    slot_rank = jnp.sum(jnp.cumsum(hits, axis=0) * hits, axis=1) - 1
    slot_index = picked * capacity + slot_rank
    place = (jnp.arange(slots, dtype=jnp.int32)[:, None] == slot_index[None, :]).astype(BF16)
    cotangent = result_cotangent_array[0]

    def to_slots(values):
        return jnp.dot(place, values, preferred_element_type=F32).astype(BF16)

    def from_slots(values):
        return dot32(place, values, (((0,), (0,))))

    grad_slots = exchange_slots(to_slots(cotangent))
    arrived = exchange_slots(to_slots(mid_low))

    project = jnp.dot(arrived, router, preferred_element_type=F32)
    unit_rows, inverse_rows, share_rows = unit_of(project, -1)
    unit_columns, inverse_columns, share_columns = unit_of(embed, 0)
    logits = jnp.dot(unit_rows, unit_columns, precision=HIGHEST) / ROUTER_HEAT
    raised = jnp.exp(logits - jnp.max(logits, axis=-1, keepdims=True))
    chances = raised / jnp.sum(raised, axis=-1, keepdims=True)
    mine = (jnp.arange(ctx_count, dtype=jnp.int32) == expert_at).astype(F32)[None, :]
    gate = jnp.sum(chances * mine, axis=-1, keepdims=True)

    first, second = arrived[:, :share], arrived[:, share:]
    rows_own = jnp.where(f_at == 0, first, second)
    rows_other = jnp.where(f_at == 0, second, first)
    pre_act = jnp.dot(rows_own, widen_own, preferred_element_type=F32) + jnp.dot(
        rows_other, widen_other, preferred_element_type=F32
    )
    bell = 0.5 * (1.0 + lax.erf(pre_act * ROOT_HALF))
    hidden = (pre_act * bell).astype(BF16)
    slope = bell + pre_act * jnp.exp(-0.5 * pre_act * pre_act) / ROOT_TWO_PI
    made = (
        jnp.dot(hidden[:, :half_ff], shrink_own, preferred_element_type=F32)
        + jnp.dot(hidden[:, half_ff:], shrink_other, preferred_element_type=F32)
    ).astype(BF16)
    made32, grad32 = made.astype(F32), grad_slots.astype(F32)
    scaled_rows = exchange_slots((gate * made32).astype(BF16))
    grad_made = (gate * grad32).astype(BF16)
    grad_gate = jnp.sum(grad32 * made32, axis=-1, keepdims=True)
    grad_hidden = jnp.concatenate(
        [dot32(grad_made, shrink_own, (((1,), (1,)))), dot32(grad_made, shrink_other, (((1,), (1,))))], axis=1
    )
    grad_pre = (grad_hidden * slope).astype(BF16)
    back_own = dot32(grad_pre, widen_own, (((1,), (1,))))
    back_other = dot32(grad_pre, widen_other, (((1,), (1,))))
    grad_inputs = jnp.where(
        f_at == 0,
        jnp.concatenate([back_own, back_other], axis=1),
        jnp.concatenate([back_other, back_own], axis=1),
    ).astype(BF16)

    grad_logits = grad_gate * gate * (mine - chances) / ROUTER_HEAT
    grad_unit = lax.dot_general(
        grad_logits, unit_columns, (((1,), (1,)), ((), ())), precision=HIGHEST
    )
    grad_project = unit_back(unit_rows, inverse_rows, share_rows, grad_unit, -1)
    grad_columns = lax.dot_general(
        unit_rows, grad_logits, (((0,), (0,)), ((), ())), precision=HIGHEST
    )
    grad_embed_own = unit_back(unit_columns, inverse_columns, share_columns, grad_columns, 0)
    grad_router_own = lax.dot_general(
        grad_project, arrived.astype(F32), (((0,), (0,)), ((), ())), precision=HIGHEST
    )
    grad_route_in = lax.dot_general(
        grad_project, router.astype(F32), (((1,), (1,)), ((), ())), precision=HIGHEST
    )
    grad_back = exchange_slots((grad_inputs.astype(F32) + grad_route_in).astype(BF16))

    grad_widen_other = swap(dot32(rows_other, grad_pre, (((0,), (0,)))).astype(BF16))
    grad_widen_own = dot32(rows_own, grad_pre, (((0,), (0,))))
    grad_shrink_other = swap(
        after(dot32(hidden[:, half_ff:], grad_made, (((0,), (0,)))).astype(BF16), grad_widen_other)
    )
    grad_shrink_own = dot32(hidden[:, :half_ff], grad_made, (((0,), (0,))))

    out = residual + from_slots(scaled_rows)
    grad_mid = from_slots(grad_back)
    grad_residual = cotangent.astype(F32) + norm_back(unit_mid, scale_mid, grad_mid * gain_mid)
    grad_gain_mid = jnp.sum(grad_mid * unit_mid, axis=0)
    grad_res_low = grad_residual.astype(BF16)
    grad_context_t = dot32(final_map, grad_res_low, (((1,), (1,)))).astype(BF16)
    grad_blocks = roll_blocks(grad_context_t.reshape(GROUPS, group_width, row_count), z_at)
    grad_t = jnp.concatenate(
        [grad_blocks[k] if k == 0 else shift(grad_blocks[k], "z", GROUPS, k) for k in range(GROUPS)], axis=1
    )

    pieces = jnp.concatenate([near, far], axis=0)
    grad_query, grad_value, grad_key = [], [], []
    for head in range(heads):
        grad_q, grad_kv = attend_back(head, query_t, onehot, grad_t, out_heads, lse, pieces, scale2, heads)
        for bit in range(bits):
            halves = grad_kv.reshape(-1, 2, *grad_kv.shape[1:])
            moved = across(halves[:, 1], 1 << bit)
            grad_kv = (halves[:, 0].astype(F32) + moved.astype(F32)).astype(BF16)
        grad_query.append(grad_q)
        grad_value.append(grad_kv[0, :HD])
        grad_key.append(grad_kv[0, HD:])
    grad_joined_t = jnp.concatenate(grad_query + grad_key + grad_value, axis=0)

    def halve(value):
        value = value.reshape(2, *([2] * bits), -1, value.shape[-1])
        for bit in range(bits):
            own_bit = (r_at >> bit) & 1
            sent = lax.dynamic_index_in_dim(value, 1 - own_bit, 1, keepdims=False)
            kept = lax.dynamic_index_in_dim(value, own_bit, 1, keepdims=False)
            value = (kept.astype(F32) + across(sent, 1 << bit).astype(F32)).astype(BF16)
        sent = lax.dynamic_index_in_dim(value, 1 - f_at, 0, keepdims=False)
        kept = lax.dynamic_index_in_dim(value, f_at, 0, keepdims=False)
        return kept.astype(F32) + swap(sent).astype(F32)

    def double(value):
        for bit in range(bits - 1, -1, -1):
            own_bit = (r_at >> bit) & 1
            value = pair_order(value, across(value, 1 << bit), own_bit)
        return value

    grad_final_part = halve(dot32(context_t, grad_res_low, (((1,), (0,)))).astype(BF16))
    for bit in (1, 2):
        grad_final_part = grad_final_part + flip(grad_final_part, "z", GROUPS, bit)
    grad_final = double(grad_final_part.astype(BF16)).astype(F32)

    grad_maps_part = halve(
        dot32(normed_low, grad_joined_t, (((0,), (1,)))).astype(BF16)
    ).astype(BF16)
    grad_maps_groups = roll_blocks(
        jnp.stack([grad_maps_part if k == 0 else shift(grad_maps_part, "z", GROUPS, k) for k in range(GROUPS)][::-1]),
        (GROUPS - 1 - z_at) % GROUPS,
    )
    part_rows = grad_maps_part.shape[0]
    grad_maps = (
        double(
            jnp.transpose(grad_maps_groups.reshape(GROUPS, part_rows, 3, group_width), (1, 2, 0, 3)).reshape(
                part_rows, 3 * width
            )
        )
    ).astype(F32)
    grad_ln1 = jnp.sum(grad_maps * asker_lookup_content_maps.astype(F32), axis=1) / mixer_scaling_factor.astype(F32)

    small = jnp.concatenate(
        [
            grad_router_own,
            jnp.pad(grad_embed_own, ((0, 0), (0, width - grad_embed_own.shape[1]))),
            jnp.pad(grad_gain_mid[None], ((0, 7), (0, 0))),
        ],
        axis=0,
    )
    for bit in range(bits):
        small = small + across(small, 1 << bit)
    small = small + swap(small)
    for bit in (1, 2):
        small = small + flip(small, "z", GROUPS, bit)
    route = grad_router_own.shape[0]
    own_columns = lax.dynamic_slice_in_dim(small, f_at * share, share, 1)
    grad_router = own_columns[:route].T
    grad_ln2 = own_columns[2 * route]
    embed_share = route // fsdp_count
    grad_embed = lax.dynamic_slice_in_dim(
        small[route : 2 * route, : grad_embed_own.shape[1]], f_at * embed_share, embed_share, 0
    )

    joined_blocks = grad_joined_t.reshape(3 * group_width, GROUPS, row_count)
    joined_parts = [
        joined_blocks[:, k] if k == 0 else shift(joined_blocks[:, k], "z", GROUPS, -k) for k in range(GROUPS)
    ]
    joined_own = roll_blocks(jnp.stack(joined_parts), (GROUPS - z_at) % GROUPS)
    joined_own = jnp.transpose(
        joined_own.reshape(GROUPS, 3, group_width, row_count), (1, 0, 2, 3)
    ).reshape(3 * width, row_count)
    grad_normed_in = dot32(joined_own, maps_full, (((0,), (1,))))
    unit_in, scale_in = norm_parts(x32)
    grad_input = grad_residual + norm_back(unit_in, scale_in, grad_normed_in * gain_in)

    turned = jnp.concatenate([grad_widen_other[:, half_ff:], grad_widen_other[:, :half_ff]], axis=1)
    grad_up = swap_columns(grad_widen_own + turned.astype(F32))
    grad_down = grad_shrink_own + grad_shrink_other.astype(F32)
    return (
        out[None].astype(BF16),
        grad_input[None],
        grad_ln1,
        grad_maps,
        grad_final,
        grad_ln2,
        grad_router,
        grad_embed,
        grad_up[None],
        grad_down[None],
    )


def solution(mesh):
    ctx_count, fsdp_count = mesh.shape["ctx"], mesh.shape["fsdp"]
    inner = Mesh(mesh.devices.reshape(GROUPS, ctx_count // GROUPS, fsdp_count), ("z", "r", "fsdp"))
    ctx = ("z", "r")
    tokens = P("fsdp", ctx, None)
    expert = P(ctx, "fsdp", None)
    halves, halves2 = P("fsdp"), P("fsdp", None)
    return jax.shard_map(
        functools.partial(body, ctx_count, fsdp_count),
        mesh=inner,
        in_specs=(
            tokens, halves, halves2, halves2, halves, halves2, halves2, expert, expert,
            P("fsdp", ctx), tokens, tokens,
        ),
        out_specs=(
            tokens, tokens, halves, halves2, halves2, halves, halves2, halves2, expert, expert,
        ),
        check_vma=False,
    )
```

time: 1110 us -> 532 us (0.48)
  matrix products: 282 us -> 63.5 us
  blocking collectives: 166 us -> 0 us
  local copies, waits for them, and re-layouts: 164 us -> 48.8 us
  waiting for transfers between devices: 321 us -> 214 us
  starting transfers between devices: 13.9 us -> 94.2 us
  loops' own time: 76.6 us -> 0 us
  Pallas kernels: 0 us -> 56.9 us
  other arithmetic: 60.8 us -> 44.9 us
  between operations: 15 us -> 2.49 us
    dot_general x74 -> x28, matrix products: 282 us -> 63.5 us  [the longest x16 39.3 us: dot32(): lax.dot_general(left, right, (dims, ((), ())), preferred_element_type=F32)]
    ppermute x0 -> x56, waiting for transfers between devices: none -> 174 us  [the longest x38 118 us: flip(): return lax.ppermute(value, axis, [(at, at ^ bit) for at in range(size)])]
    all_gather x8 -> x0, waiting for transfers between devices: 141 us -> none  [the longest x1 54.1 us: body(): value_piece = lax.all_gather(value_rows, 'ctx', axis=0, tiled=True)]
    psum x1 -> x0, waiting for transfers between devices: 133 us -> none  [body(): lax.psum((grad_gain_in, grad_qkv_full, grad_out_full, grad_gain_mid, grad...]
    dynamic_slice x78 -> x10, local copies, waits for them, and re-layouts: 93.3 us -> 5.8 us  [the longest x4 3.04 us: roll_blocks(): lax.dynamic_slice_in_dim(jnp.concatenate([blocks, blocks], axis=0), start...]
    all_gather x7 -> x0, blocking collectives: 86.6 us -> none  [the longest x1 24.7 us: body(): lax.all_gather(lse_rows, 'ctx', axis=0, tiled=True)]
    another operation x27 -> x0, loops' own time: 76.6 us -> none  [the longest x3 75.3 us: over_blocks(): lax.scan(advance, state, jnp.arange(piece_rows // block_rows, dtype=jnp.i...]
    ppermute x0 -> x56, starting transfers between devices: none -> 72.9 us  [the longest x38 35.2 us: flip(): return lax.ppermute(value, axis, [(at, at ^ bit) for at in range(size)])]
  transfers between devices with their start and end apart: 14 -> 60, of which waited for: 8 -> 27; matrix products, arithmetic and copies ran while one was open for 45% -> 23% of each run, Pallas kernels for 0% -> 11%
where the time goes in v1:
time: 532 us; the launch traced here: 525 us
  waiting for transfers between devices  214 us (40%)
  starting transfers between devices  94.2 us (18%)
  matrix products  63.5 us (12%)
  Pallas kernels  56.9 us (11%)
  local copies, waits for them, and re-layouts  48.8 us (9%)
  other arithmetic  44.9 us (8%)
    ppermute x38, waiting for transfers between devices, flip(): return lax.ppermute(value, axis, [(at, at ^ bit) for at in range(size)])  118 us
    all_to_all x4, waiting for transfers between devices, exchange_slots(): lax.all_to_all(rows.reshape(ctx_count, capacity, -1), ('z', 'r'), split_a...  40.1 us
    dot_general x16, matrix products, dot32(): lax.dot_general(left, right, (dims, ((), ())), preferred_element_type=F32)  39.3 us
    ppermute x12, waiting for transfers between devices, shift(): lax.ppermute(value, axis, [(at, (at + by) % size) for at in range(size)])  36.2 us
    ppermute x38, starting transfers between devices, flip(): return lax.ppermute(value, axis, [(at, at ^ bit) for at in range(size)])  35.2 us
    pallas_call x3, Pallas kernels, attend_back(): pl.pallas_call(functools.partial(backward_kernel, scale2), grid=(count,),...  33.2 us
    ppermute x12, starting transfers between devices, shift(): lax.ppermute(value, axis, [(at, (at + by) % size) for at in range(size)])  26.7 us
    pallas_call x2, Pallas kernels, attend(): pl.pallas_call(functools.partial(forward_kernel, scale2, last), grid=(hea...  23.7 us
  transfers between devices with their start and end apart: 60, of which 27 were waited for; matrix products, arithmetic and copies ran while one was open for 23% of the time, Pallas kernels for 11%

profile of v1, /device:TPU:0, one launch (start us, length us, event | category | flops | bytes accessed | tf_op | source)
XLA Modules:
  0.0 525.4 jit_solution(14758239242930289603)
XLA Ops:
  3.1 5.8 %collective-permute-start.1 = (bf16[272,768]{1,0:T(8,128)(2,1)}, bf16[272,768]{1,0:T(8,128)(2,1)}, u32[]{:S(2)}, u32[]{:S(2)}) collective-permute-start(bf16[272,768]{1,0:T(8,128)(2,1)} %fusion.66), channel_id=1, source_target_pairs={{0,8},{8,16},{16,24},{1,9},{9,17},{17,25},{2,10},{10,18},{18,26},{... | collective-permute-start | bytes 1253384 | tf_op jit(solution)/shard_map/ppermute | solution.py:243
  10.2 3.9 copy.60
  26.1 8.5 %collective-permute-done.3 = bf16[272,768]{1,0:T(8,128)(2,1)S(1)} collective-permute-done((bf16[272,768]{1,0:T(8,128)(2,1)}, bf16[272,768]{1,0:T(8,128)(2,1)S(1)}, u32[]{:S(2)}, u32[]{:S(2)}) %collective-permute-start.3) | collective-permute-done | bytes 417824 | tf_op jit(solution)/shard_map/ppermute | solution.py:244
  37.4 8.2 %collective-permute-done.4 = bf16[272,768]{1,0:T(8,128)(2,1)S(1)} collective-permute-done((bf16[272,768]{1,0:T(8,128)(2,1)S(1)}, bf16[272,768]{1,0:T(8,128)(2,1)S(1)}, u32[]{:S(2)}, u32[]{:S(2)}) %collective-permute-start.4) | collective-permute-done | bytes 417824 | tf_op jit(solution)/shard_map/ppermute | solution.py:244
  54.6 4.5 collective-permute-done.14
  69.1 11.8 %shard_map.195 = (f32[3,1,1024]{2,1,0:T(1,128)S(1)}, f32[3,80,1024]{2,1,0:T(8,128)S(1)}) custom-call(bf16[192,1024]{1,0:T(8,128)(2,1)S(1)} %slice.254.q_ref, bf16[16,1024]{1,0:T(8,128)(2,1)S(1)} %fusion.82.oh_ref, bf16[2,400,1024]{2,1,0:T(8,128)(2,1)S(1)} %pad_maximum_fusion.2.k_ref.v_ref.mk_ref, ...), custom_call_target="tpu_custom_call" | custom-call | flops 6442450944 | bytes 1572864 | tf_op jit(solution)/shard_map/pallas_call | solution.py:100
  82.3 11.9 %shard_map.196 = (f32[3,64,1024]{2,1,0:T(8,128)S(1)}, f32[3,1,1024]{2,1,0:T(1,128)S(1)}) custom-call(bf16[192,1024]{1,0:T(8,128)(2,1)S(1)} %slice.254.q_ref, bf16[16,1024]{1,0:T(8,128)(2,1)S(1)} %fusion.82.oh_ref, bf16[2,400,1024]{2,1,0:T(8,128)(2,1)S(1)} %maximum_bitcast_fusion.k_ref.v_ref.mk_ref, ...), custom_call_target="tpu_custom_call" | custom-call | flops 6442450944 | bytes 1572864 | tf_op jit(solution)/shard_map/pallas_call | solution.py:100
  102.2 11.0 %collective-permute-start.13 = (bf16[192,256]{1,0:T(8,128)(2,1)S(1)}, bf16[192,256]{1,0:T(8,128)(2,1)S(1)}, u32[]{:S(2)}, u32[]{:S(2)}) collective-permute-start(bf16[192,256]{1,0:T(8,128)(2,1)S(1)} %bitcast.318), channel_id=1, source_target_pairs={{0,8},{8,16},{16,24},{24,0},{1,9},{9,17},{17,25},{25,1},{2,10},{10... | collective-permute-start | bytes 294920 | tf_op jit(solution)/shard_map/ppermute | solution.py:229
  113.2 5.8 %collective-permute-done.13 = bf16[192,256]{1,0:T(8,128)(2,1)S(1)} collective-permute-done((bf16[192,256]{1,0:T(8,128)(2,1)S(1)}, bf16[192,256]{1,0:T(8,128)(2,1)S(1)}, u32[]{:S(2)}, u32[]{:S(2)}) %collective-permute-start.13) | collective-permute-done | bytes 98336 | tf_op jit(solution)/shard_map/ppermute | solution.py:229
  122.2 4.3 all-to-all-start
  131.2 14.0 %all-to-all-done = bf16[16,32,768]{2,1,0:T(8,128)(2,1)} async-done(((bf16[16,32,768]{2,1,0:T(8,128)(2,1)}), bf16[16,32,768]{2,1,0:T(8,128)(2,1)}, u32[]{:S(2)}, u32[]{:S(2)}) %all-to-all-start) | async-done | bytes 786464 | tf_op jit(solution)/shard_map/all_to_all | solution.py:298
  145.2 5.5 %all-to-all-start.2 = ((bf16[16,32,768]{2,1,0:T(8,128)(2,1)}), bf16[16,32,768]{2,1,0:T(8,128)(2,1)}, u32[]{:S(2)}, u32[]{:S(2)}) async-start(bf16[16,32,768]{2,1,0:T(8,128)(2,1)} %bitcast.303), calls=%async_computation.2 | async-start | bytes 1572864 | tf_op jit(solution)/shard_map/all_to_all | solution.py:298
  157.7 11.7 %all-to-all-done.2 = bf16[16,32,768]{2,1,0:T(8,128)(2,1)} async-done(((bf16[16,32,768]{2,1,0:T(8,128)(2,1)}), bf16[16,32,768]{2,1,0:T(8,128)(2,1)}, u32[]{:S(2)}, u32[]{:S(2)}) %all-to-all-start.2) | async-done | bytes 786464 | tf_op jit(solution)/shard_map/all_to_all | solution.py:298
  177.1 27.9 %collective-permute-done.19 = bf16[1536,768]{1,0:T(8,128)(2,1)} collective-permute-done((bf16[1536,768]{1,0:T(8,128)(2,1)}, bf16[1536,768]{1,0:T(8,128)(2,1)}, u32[]{:S(2)}, u32[]{:S(2)}) %collective-permute-start.19) | collective-permute-done | bytes 2359328 | tf_op jit(solution)/shard_map/ppermute | solution.py:233
  208.2 6.4 %fusion.5 = (bf16[512,3072]{1,0:T(8,128)(2,1)S(1)}, bf16[512,3072]{1,0:T(8,128)(2,1)S(1)}) fusion(f32[512,1536]{1,0:T(8,128)S(1)} %fusion.142, f32[512,1536]{1,0:T(8,128)S(1)} %fusion.120, f32[512,3072]{1,0:T(8,128)S(1)} %fusion.84, bf16[384,3072]{1,0:T(8,128)(2,1)} %collective-permute-done.18, pred[]{:T(512)S(6)} %eq.104, bf16[512,768]{1,0:T(8,128)(2,1)} %bitcast.19), kind=kOutput, calls=%fused_computation.6 | convolution fusion | flops 1230176256 | bytes 22020096 | tf_op jit(solution)/shard_map/dot_general | solution.py:405
  217.4 4.3 fusion.21
  229.4 6.0 %all-to-all-start.3 = ((bf16[16,32,768]{2,1,0:T(8,128)(2,1)}), bf16[16,32,768]{2,1,0:T(8,128)(2,1)}, u32[]{:S(2)}, u32[]{:S(2)}) async-start(bf16[16,32,768]{2,1,0:T(8,128)(2,1)} %bitcast.301), calls=%async_computation.3 | async-start | bytes 1572864 | tf_op jit(solution)/shard_map/all_to_all | solution.py:298
  237.9 5.0 convolution_convert_fusion
  254.2 5.5 %all-to-all-start.1 = ((bf16[16,32,768]{2,1,0:T(8,128)(2,1)}), bf16[16,32,768]{2,1,0:T(8,128)(2,1)}, u32[]{:S(2)}, u32[]{:S(2)}) async-start(bf16[16,32,768]{2,1,0:T(8,128)(2,1)} %bitcast.22), calls=%async_computation.1 | async-start | bytes 1572864 | tf_op jit(solution)/shard_map/all_to_all | solution.py:298
  266.1 12.3 %all-to-all-done.1 = bf16[16,32,768]{2,1,0:T(8,128)(2,1)} async-done(((bf16[16,32,768]{2,1,0:T(8,128)(2,1)}), bf16[16,32,768]{2,1,0:T(8,128)(2,1)}, u32[]{:S(2)}, u32[]{:S(2)}) %all-to-all-start.1) | async-done | bytes 786464 | tf_op jit(solution)/shard_map/all_to_all | solution.py:298
  288.5 7.0 %collective-permute-done.21 = bf16[192,256]{1,0:T(8,128)(2,1)S(1)} collective-permute-done((bf16[192,256]{1,0:T(8,128)(2,1)S(1)}, bf16[192,256]{1,0:T(8,128)(2,1)S(1)}, u32[]{:S(2)}, u32[]{:S(2)}) %collective-permute-start.21) | collective-permute-done | bytes 98336 | tf_op jit(solution)/shard_map/ppermute | solution.py:229
  295.5 11.1 %shard_map.197 = (bf16[64,1024]{1,0:T(8,128)(2,1)S(1)}, bf16[4,128,1024]{2,1,0:T(8,128)(2,1)S(1)}) custom-call(bf16[192,1024]{1,0:T(8,128)(2,1)S(1)} %slice.254.q_ref, bf16[16,1024]{1,0:T(8,128)(2,1)S(1)} %fusion.82.oh_ref, bf16[192,1024]{1,0:T(8,128)(2,1)S(1)} %pad_maximum_fusion.4.g_ref, f32[3,64,1024]{2,1,0:T(8,128)S(1)} %get-tuple-element.39.o_ref, ...), custom_call_target="tpu_custom_call" | custom-call | flops 10737418240 | bytes 2097152 | tf_op jit(solution)/shard_map/pallas_call | solution.py:172
  306.6 11.1 %shard_map.198 = (bf16[64,1024]{1,0:T(8,128)(2,1)S(1)}, bf16[4,128,1024]{2,1,0:T(8,128)(2,1)S(1)}) custom-call(bf16[192,1024]{1,0:T(8,128)(2,1)S(1)} %slice.254.q_ref, bf16[16,1024]{1,0:T(8,128)(2,1)S(1)} %fusion.82.oh_ref, bf16[192,1024]{1,0:T(8,128)(2,1)S(1)} %pad_maximum_fusion.4.g_ref, f32[3,64,1024]{2,1,0:T(8,128)S(1)} %get-tuple-element.39.o_ref, ...), custom_call_target="tpu_custom_call" | custom-call | flops 10737418240 | bytes 2097152 | tf_op jit(solution)/shard_map/pallas_call | solution.py:172
  317.7 11.1 %shard_map.199 = (bf16[64,1024]{1,0:T(8,128)(2,1)S(1)}, bf16[4,128,1024]{2,1,0:T(8,128)(2,1)S(1)}) custom-call(bf16[192,1024]{1,0:T(8,128)(2,1)S(1)} %slice.254.q_ref, bf16[16,1024]{1,0:T(8,128)(2,1)S(1)} %fusion.82.oh_ref, bf16[192,1024]{1,0:T(8,128)(2,1)S(1)} %pad_maximum_fusion.4.g_ref, f32[3,64,1024]{2,1,0:T(8,128)S(1)} %get-tuple-element.39.o_ref, ...), custom_call_target="tpu_custom_call" | custom-call | flops 10737418240 | bytes 2097152 | tf_op jit(solution)/shard_map/pallas_call | solution.py:172
  349.4 6.6 %collective-permute-done.53 = f32[40,768]{1,0:T(8,128)S(1)} collective-permute-done((f32[40,768]{1,0:T(8,128)S(1)}, f32[40,768]{1,0:T(8,128)S(1)}, u32[]{:S(2)}, u32[]{:S(2)}) %collective-permute-start.53) | collective-permute-done | bytes 122912 | tf_op jit(solution)/shard_map/ppermute | solution.py:233
  363.5 8.2 %collective-permute-done.24 = bf16[1,128,1024]{2,1,0:T(8,128)(2,1)S(1)} collective-permute-done((bf16[1,128,1024]{2,1,0:T(8,128)(2,1)S(1)}, bf16[1,128,1024]{2,1,0:T(8,128)(2,1)S(1)}, u32[]{:S(2)}, u32[]{:S(2)}) %collective-permute-start.24) | collective-permute-done | bytes 262176 | tf_op jit(solution)/shard_map/ppermute | solution.py:233
  371.8 5.5 %collective-permute-done.26 = bf16[1,128,1024]{2,1,0:T(8,128)(2,1)S(1)} collective-permute-done((bf16[1,128,1024]{2,1,0:T(8,128)(2,1)S(1)}, bf16[1,128,1024]{2,1,0:T(8,128)(2,1)S(1)}, u32[]{:S(2)}, u32[]{:S(2)}) %collective-permute-start.26) | collective-permute-done | bytes 262176 | tf_op jit(solution)/shard_map/ppermute | solution.py:233
  377.6 4.6 collective-permute-done.28
  427.0 37.5 %collective-permute-done.36 = bf16[96,576]{1,0:T(8,128)(2,1)S(1)} collective-permute-done((bf16[96,576]{1,0:T(8,128)(2,1)S(1)}, bf16[96,576]{1,0:T(8,128)(2,1)S(1)}, u32[]{:S(2)}, u32[]{:S(2)}) %collective-permute-start.36) | collective-permute-done | bytes 110624 | tf_op jit(solution)/shard_map/ppermute | solution.py:233
  471.7 20.3 %collective-permute-done.38 = bf16[96,576]{1,0:T(8,128)(2,1)S(1)} collective-permute-done((bf16[96,576]{1,0:T(8,128)(2,1)S(1)}, bf16[96,576]{1,0:T(8,128)(2,1)S(1)}, u32[]{:S(2)}, u32[]{:S(2)}) %collective-permute-start.38) | collective-permute-done | bytes 110624 | tf_op jit(solution)/shard_map/ppermute | solution.py:229
  506.6 6.3 %collective-permute-done.40 = bf16[96,2304]{1,0:T(8,128)(2,1)S(1)} collective-permute-done((bf16[96,2304]{1,0:T(8,128)(2,1)}, bf16[96,2304]{1,0:T(8,128)(2,1)S(1)}, u32[]{:S(2)}, u32[]{:S(2)}) %collective-permute-start.40) | collective-permute-done | bytes 442400 | tf_op jit(solution)/shard_map/ppermute | solution.py:233
  520.6 4.6 add_bitcast_fusion
  (415 shorter events, 214.7 us)
Async XLA Ops:
  15.2 20.7 %collective-permute-start = (bf16[384,576]{0,1:T(8,128)(2,1)S(1)}, bf16[384,576]{0,1:T(8,128)(2,1)}, u32[]{:S(2)}, u32[]{:S(2)}) collective-permute-start(bf16[384,576]{0,1:T(8,128)(2,1)S(1)} %bitcast.313), channel_id=1, source_target_pairs={{0,1},{1,0},{2,3},{3,2},{4,5},{5,4},{6,7},{7,6},{8,9},{9,8},{10,11... | collective-permute-start | bytes 1327112 | tf_op jit(solution)/shard_map/ppermute | solution.py:233
  16.8 19.0 %collective-permute-start.7 = (bf16[2,384]{1,0:T(2,128)(2,1)S(1)}, bf16[2,384]{1,0:T(2,128)(2,1)S(1)}, u32[]{:S(2)}, u32[]{:S(2)}) collective-permute-start(bf16[2,384]{1,0:T(2,128)(2,1)S(1)} %pad_maximum_fusion.5), channel_id=1, source_target_pairs={{0,1},{1,0},{2,3},{3,2},{4,5},{5,4},{6,7},{7,6},{8,9},{9,8},{10,11... | collective-permute-start | bytes 4616 | tf_op jit(solution)/shard_map/ppermute | solution.py:233
  50.6 17.0 %collective-permute-start.8 = (bf16[1,400,1024]{2,1,0:T(8,128)(2,1)S(1)}, bf16[1,400,1024]{2,1,0:T(8,128)(2,1)S(1)}, u32[]{:S(2)}, u32[]{:S(2)}) collective-permute-start(bf16[1,400,1024]{2,1,0:T(8,128)(2,1)S(1)} %maximum_bitcast_fusion.1), channel_id=1, source_target_pairs={{0,4},{2,6},{4,0},{6,2},{1,5},{3,7},{5,1},{7,3},{8,12},{10,14},{12... | collective-permute-start | bytes 2457608 | tf_op jit(solution)/shard_map/ppermute | solution.py:233
  62.9 88.3 %collective-permute-start.18 = (bf16[384,3072]{1,0:T(8,128)(2,1)}, bf16[384,3072]{1,0:T(8,128)(2,1)}, u32[]{:S(2)}, u32[]{:S(2)}) collective-permute-start(bf16[384,3072]{1,0:T(8,128)(2,1)} %pad_maximum_fusion.1), channel_id=1, source_target_pairs={{0,1},{1,0},{2,3},{3,2},{4,5},{5,4},{6,7},{7,6},{8,9},{9,8},{10,11... | collective-permute-start | bytes 7077896 | tf_op jit(solution)/shard_map/ppermute | solution.py:233
  102.2 16.9 %collective-permute-start.13 = (bf16[192,256]{1,0:T(8,128)(2,1)S(1)}, bf16[192,256]{1,0:T(8,128)(2,1)S(1)}, u32[]{:S(2)}, u32[]{:S(2)}) collective-permute-start(bf16[192,256]{1,0:T(8,128)(2,1)S(1)} %bitcast.318), channel_id=1, source_target_pairs={{0,8},{8,16},{16,24},{24,0},{1,9},{9,17},{17,25},{25,1},{2,10},{10... | collective-permute-start | bytes 294920 | tf_op jit(solution)/shard_map/ppermute | solution.py:229
  122.2 23.0 %all-to-all-start = ((bf16[16,32,768]{2,1,0:T(8,128)(2,1)}), bf16[16,32,768]{2,1,0:T(8,128)(2,1)}, u32[]{:S(2)}, u32[]{:S(2)}) async-start(bf16[16,32,768]{2,1,0:T(8,128)(2,1)} %bitcast.302), calls=%async_computation | async-start | bytes 1572864 | tf_op jit(solution)/shard_map/all_to_all | solution.py:298
  126.5 24.2 %collective-permute-start.17 = (bf16[8,16]{1,0:T(8,128)(2,1)S(1)}, bf16[8,16]{1,0:T(8,128)(2,1)S(1)}, u32[]{:S(2)}, u32[]{:S(2)}) collective-permute-start(bf16[8,16]{1,0:T(8,128)(2,1)S(1)} %copy-done.36), channel_id=1, source_target_pairs={{0,1},{1,0},{2,3},{3,2},{4,5},{5,4},{6,7},{7,6},{8,9},{9,8},{10,11... | collective-permute-start | bytes 776 | tf_op jit(solution)/shard_map/ppermute | solution.py:233
  128.1 27.7 %collective-permute-start.16 = (bf16[384,16]{0,1:T(8,128)(2,1)S(1)}, bf16[384,16]{0,1:T(8,128)(2,1)S(1)}, u32[]{:S(2)}, u32[]{:S(2)}) collective-permute-start(bf16[384,16]{0,1:T(8,128)(2,1)S(1)} %copy-done.38), channel_id=1, source_target_pairs={{0,1},{1,0},{2,3},{3,2},{4,5},{5,4},{6,7},{7,6},{8,9},{9,8},{10,11... | collective-permute-start | bytes 36872 | tf_op jit(solution)/shard_map/ppermute | solution.py:233
  145.2 24.2 %all-to-all-start.2 = ((bf16[16,32,768]{2,1,0:T(8,128)(2,1)}), bf16[16,32,768]{2,1,0:T(8,128)(2,1)}, u32[]{:S(2)}, u32[]{:S(2)}) async-start(bf16[16,32,768]{2,1,0:T(8,128)(2,1)} %bitcast.303), calls=%async_computation.2 | async-start | bytes 1572864 | tf_op jit(solution)/shard_map/all_to_all | solution.py:298
  151.3 53.8 %collective-permute-start.19 = (bf16[1536,768]{1,0:T(8,128)(2,1)}, bf16[1536,768]{1,0:T(8,128)(2,1)}, u32[]{:S(2)}, u32[]{:S(2)}) collective-permute-start(bf16[1536,768]{1,0:T(8,128)(2,1)} %bitcast.322), channel_id=1, source_target_pairs={{0,1},{1,0},{2,3},{3,2},{4,5},{5,4},{6,7},{7,6},{8,9},{9,8},{10,11... | collective-permute-start | bytes 7077896 | tf_op jit(solution)/shard_map/ppermute | solution.py:233
  229.4 24.8 %all-to-all-start.3 = ((bf16[16,32,768]{2,1,0:T(8,128)(2,1)}), bf16[16,32,768]{2,1,0:T(8,128)(2,1)}, u32[]{:S(2)}, u32[]{:S(2)}) async-start(bf16[16,32,768]{2,1,0:T(8,128)(2,1)} %bitcast.301), calls=%async_computation.3 | async-start | bytes 1572864 | tf_op jit(solution)/shard_map/all_to_all | solution.py:298
  236.4 23.3 %collective-permute-start.32 = (bf16[192,2304]{1,0:T(8,128)(2,1)}, bf16[192,2304]{1,0:T(8,128)(2,1)}, u32[]{:S(2)}, u32[]{:S(2)}) collective-permute-start(bf16[192,2304]{1,0:T(8,128)(2,1)} %constant_dynamic-slice_fusion.4), channel_id=1, source_target_pairs={{0,1},{1,0},{2,3},{3,2},{4,5},{5,4},{6,7},{7,6},{8,9},{9,8},{10,11... | collective-permute-start | bytes 2654216 | tf_op jit(solution)/shard_map/ppermute | solution.py:233
  243.0 155.8 %collective-permute-start.54 = (bf16[384,3072]{1,0:T(8,128)(2,1)}, bf16[384,3072]{1,0:T(8,128)(2,1)}, u32[]{:S(2)}, u32[]{:S(2)}) collective-permute-start(bf16[384,3072]{1,0:T(8,128)(2,1)} %convolution_convert_fusion), channel_id=1, source_target_pairs={{0,1},{1,0},{2,3},{3,2},{4,5},{5,4},{6,7},{7,6},{8,9},{9,8},{10,11... | collective-permute-start | bytes 7077896 | tf_op jit(solution)/shard_map/ppermute | solution.py:233
  254.2 24.3 %all-to-all-start.1 = ((bf16[16,32,768]{2,1,0:T(8,128)(2,1)}), bf16[16,32,768]{2,1,0:T(8,128)(2,1)}, u32[]{:S(2)}, u32[]{:S(2)}) async-start(bf16[16,32,768]{2,1,0:T(8,128)(2,1)} %bitcast.22), calls=%async_computation.1 | async-start | bytes 1572864 | tf_op jit(solution)/shard_map/all_to_all | solution.py:298
  259.7 81.4 %collective-permute-start.33 = (bf16[192,2304]{1,0:T(8,128)(2,1)}, bf16[192,2304]{1,0:T(8,128)(2,1)}, u32[]{:S(2)}, u32[]{:S(2)}) collective-permute-start(bf16[192,2304]{1,0:T(8,128)(2,1)} %collective-permute-done.32), channel_id=1, source_target_pairs={{0,2},{2,0},{4,6},{6,4},{1,3},{3,1},{5,7},{7,5},{8,10},{10,8},{12,... | collective-permute-start | bytes 2654216 | tf_op jit(solution)/shard_map/ppermute | solution.py:233
  288.4 58.6 %collective-permute-start.42 = (bf16[2,2,96,768]{3,2,0,1:T(8,128)(2,1)S(1)}, bf16[2,2,96,768]{3,2,0,1:T(8,128)(2,1)S(1)}, u32[]{:S(2)}, u32[]{:S(2)}) collective-permute-start(bf16[2,2,96,768]{3,2,0,1:T(8,128)(2,1)S(1)} %bitcast.312), channel_id=1, source_target_pairs={{0,2},{2,0},{4,6},{6,4},{1,3},{3,1},{5,7},{7,5},{8,10},{10,8},{12,... | collective-permute-start | bytes 1769480 | tf_op jit(solution)/shard_map/ppermute | solution.py:233
  295.5 35.3 %collective-permute-start.49 = (f32[40,768]{1,0:T(8,128)S(1)}, f32[40,768]{1,0:T(8,128)S(1)}, u32[]{:S(2)}, u32[]{:S(2)}) collective-permute-start(f32[40,768]{1,0:T(8,128)S(1)} %select_maximum_fusion), channel_id=1, source_target_pairs={{0,2},{2,0},{4,6},{6,4},{1,3},{3,1},{5,7},{7,5},{8,10},{10,8},{12,... | collective-permute-start | bytes 368648 | tf_op jit(solution)/shard_map/ppermute | solution.py:233
  329.5 29.8 %collective-permute-start.23 = (bf16[2,128,1024]{2,1,0:T(8,128)(2,1)S(1)}, bf16[2,128,1024]{2,1,0:T(8,128)(2,1)S(1)}, u32[]{:S(2)}, u32[]{:S(2)}) collective-permute-start(bf16[2,128,1024]{2,1,0:T(8,128)(2,1)S(1)} %slice_bitcast_fusion.4), channel_id=1, source_target_pairs={{0,2},{2,0},{4,6},{6,4},{1,3},{3,1},{5,7},{7,5},{8,10},{10,8},{12,... | collective-permute-start | bytes 1572872 | tf_op jit(solution)/shard_map/ppermute | solution.py:233
  341.1 19.1 %collective-permute-start.25 = (bf16[2,128,1024]{2,1,0:T(8,128)(2,1)S(1)}, bf16[2,128,1024]{2,1,0:T(8,128)(2,1)S(1)}, u32[]{:S(2)}, u32[]{:S(2)}) collective-permute-start(bf16[2,128,1024]{2,1,0:T(8,128)(2,1)S(1)} %slice_bitcast_fusion.2), channel_id=1, source_target_pairs={{0,2},{2,0},{4,6},{6,4},{1,3},{3,1},{5,7},{7,5},{8,10},{10,8},{12,... | collective-permute-start | bytes 1572872 | tf_op jit(solution)/shard_map/ppermute | solution.py:233
  356.0 41.6 %collective-permute-start.43 = (bf16[2,96,768]{2,1,0:T(8,128)(2,1)}, bf16[2,96,768]{2,1,0:T(8,128)(2,1)}, u32[]{:S(2)}, u32[]{:S(2)}) collective-permute-start(bf16[2,96,768]{2,1,0:T(8,128)(2,1)} %dynamic-slice_bitcast_fusion.1), channel_id=1, source_target_pairs={{0,4},{2,6},{4,0},{6,2},{1,5},{3,7},{5,1},{7,3},{8,12},{10,14},{12... | collective-permute-start | bytes 884744 | tf_op jit(solution)/shard_map/ppermute | solution.py:233
  360.4 16.9 %collective-permute-start.26 = (bf16[1,128,1024]{2,1,0:T(8,128)(2,1)S(1)}, bf16[1,128,1024]{2,1,0:T(8,128)(2,1)S(1)}, u32[]{:S(2)}, u32[]{:S(2)}) collective-permute-start(bf16[1,128,1024]{2,1,0:T(8,128)(2,1)S(1)} %slice_bitcast_fusion.12), channel_id=1, source_target_pairs={{0,4},{2,6},{4,0},{6,2},{1,5},{3,7},{5,1},{7,3},{8,12},{10,14},{12... | collective-permute-start | bytes 786440 | tf_op jit(solution)/shard_map/ppermute | solution.py:233
  363.0 19.2 %collective-permute-start.28 = (bf16[1,128,1024]{2,1,0:T(8,128)(2,1)}, bf16[1,128,1024]{2,1,0:T(8,128)(2,1)}, u32[]{:S(2)}, u32[]{:S(2)}) collective-permute-start(bf16[1,128,1024]{2,1,0:T(8,128)(2,1)} %slice_bitcast_fusion.10), channel_id=1, source_target_pairs={{0,4},{2,6},{4,0},{6,2},{1,5},{3,7},{5,1},{7,3},{8,12},{10,14},{12... | collective-permute-start | bytes 786440 | tf_op jit(solution)/shard_map/ppermute | solution.py:233
  391.3 17.9 %collective-permute-start.29 = (bf16[576,256]{1,0:T(8,128)(2,1)}, bf16[576,256]{1,0:T(8,128)(2,1)}, u32[]{:S(2)}, u32[]{:S(2)}) collective-permute-start(bf16[576,256]{1,0:T(8,128)(2,1)} %get-tuple-element.75), channel_id=1, source_target_pairs={{0,24},{8,0},{16,8},{24,16},{1,25},{9,1},{17,9},{25,17},{2,26},{10... | collective-permute-start | bytes 884744 | tf_op jit(solution)/shard_map/ppermute | solution.py:229
  392.6 24.2 %collective-permute-start.30 = (bf16[576,256]{1,0:T(8,128)(2,1)}, bf16[576,256]{1,0:T(8,128)(2,1)}, u32[]{:S(2)}, u32[]{:S(2)}) collective-permute-start(bf16[576,256]{1,0:T(8,128)(2,1)} %get-tuple-element.74), channel_id=1, source_target_pairs={{0,16},{8,24},{16,0},{24,8},{1,17},{9,25},{17,1},{25,9},{2,18},{10... | collective-permute-start | bytes 884744 | tf_op jit(solution)/shard_map/ppermute | solution.py:229
  392.6 25.2 %collective-permute-start.31 = (bf16[576,256]{1,0:T(8,128)(2,1)}, bf16[576,256]{1,0:T(8,128)(2,1)S(1)}, u32[]{:S(2)}, u32[]{:S(2)}) collective-permute-start(bf16[576,256]{1,0:T(8,128)(2,1)} %get-tuple-element.73), channel_id=1, source_target_pairs={{0,8},{8,16},{16,24},{24,0},{1,9},{9,17},{17,25},{25,1},{2,10},{10... | collective-permute-start | bytes 884744 | tf_op jit(solution)/shard_map/ppermute | solution.py:229
  397.6 21.2 %collective-permute-start.34 = (bf16[2,2,96,576]{3,2,1,0:T(8,128)(2,1)S(1)}, bf16[2,2,96,576]{3,2,1,0:T(8,128)(2,1)S(1)}, u32[]{:S(2)}, u32[]{:S(2)}) collective-permute-start(bf16[2,2,96,576]{3,2,1,0:T(8,128)(2,1)S(1)} %dynamic-slice_bitcast_fusion), channel_id=1, source_target_pairs={{0,2},{2,0},{4,6},{6,4},{1,3},{3,1},{5,7},{7,5},{8,10},{10,8},{12,... | collective-permute-start | bytes 1327112 | tf_op jit(solution)/shard_map/ppermute | solution.py:233
  408.2 112.4 %collective-permute-start.55 = (bf16[1536,768]{1,0:T(8,128)(2,1)}, bf16[1536,768]{1,0:T(8,128)(2,1)}, u32[]{:S(2)}, u32[]{:S(2)}) collective-permute-start(bf16[1536,768]{1,0:T(8,128)(2,1)} %convolution_convert_fusion.1), channel_id=1, source_target_pairs={{0,1},{1,0},{2,3},{3,2},{4,5},{5,4},{6,7},{7,6},{8,9},{9,8},{10,11... | collective-permute-start | bytes 7077896 | tf_op jit(solution)/shard_map/ppermute | solution.py:233
  409.2 59.5 %collective-permute-start.45 = (f32[96,768]{1,0:T(8,128)S(1)}, f32[96,768]{1,0:T(8,128)S(1)}, u32[]{:S(2)}, u32[]{:S(2)}) collective-permute-start(f32[96,768]{1,0:T(8,128)S(1)} %convert_add_fusion.11), channel_id=1, source_target_pairs={{0,8},{8,0},{16,24},{24,16},{1,9},{9,1},{17,25},{25,17},{2,10},{10... | collective-permute-start | bytes 884744 | tf_op jit(solution)/shard_map/ppermute | solution.py:233
  425.4 39.1 %collective-permute-start.36 = (bf16[96,576]{1,0:T(8,128)(2,1)S(1)}, bf16[96,576]{1,0:T(8,128)(2,1)S(1)}, u32[]{:S(2)}, u32[]{:S(2)}) collective-permute-start(bf16[96,576]{1,0:T(8,128)(2,1)S(1)} %dynamic-slice_bitcast_fusion.4), channel_id=1, source_target_pairs={{0,1},{1,0},{2,3},{3,2},{4,5},{5,4},{6,7},{7,6},{8,9},{9,8},{10,11... | collective-permute-start | bytes 331784 | tf_op jit(solution)/shard_map/ppermute | solution.py:233
  468.7 35.9 %collective-permute-start.46 = (f32[96,768]{1,0:T(8,128)S(1)}, f32[96,768]{1,0:T(8,128)}, u32[]{:S(2)}, u32[]{:S(2)}) collective-permute-start(f32[96,768]{1,0:T(8,128)S(1)} %add.261), channel_id=1, source_target_pairs={{0,16},{8,24},{16,0},{24,8},{1,17},{9,25},{17,1},{25,9},{2,18},{10... | collective-permute-start | bytes 884744 | tf_op jit(solution)/shard_map/ppermute | solution.py:233
  469.9 22.1 %collective-permute-start.38 = (bf16[96,576]{1,0:T(8,128)(2,1)S(1)}, bf16[96,576]{1,0:T(8,128)(2,1)S(1)}, u32[]{:S(2)}, u32[]{:S(2)}) collective-permute-start(bf16[96,576]{1,0:T(8,128)(2,1)S(1)} %fusion.78), channel_id=1, source_target_pairs={{0,16},{8,24},{16,0},{24,8},{1,17},{9,25},{17,1},{25,9},{2,18},{10... | collective-permute-start | bytes 331784 | tf_op jit(solution)/shard_map/ppermute | solution.py:229
  471.7 20.3 %collective-permute-start.39 = (bf16[96,576]{1,0:T(8,128)(2,1)S(1)}, bf16[96,576]{1,0:T(8,128)(2,1)S(1)}, u32[]{:S(2)}, u32[]{:S(2)}) collective-permute-start(bf16[96,576]{1,0:T(8,128)(2,1)S(1)} %fusion.78), channel_id=1, source_target_pairs={{0,8},{8,16},{16,24},{24,0},{1,9},{9,17},{17,25},{25,1},{2,10},{10... | collective-permute-start | bytes 331784 | tf_op jit(solution)/shard_map/ppermute | solution.py:229
  (80 other events, 761.0 us)
